TPU v7x, 32 devices: a whole 2x2x4 slice. The times are simulated.
32 devices in a mesh: expert: 4 (over y, x), tensor: 8 (over z, core).
Axes of the slice: x: 2, y: 2, z: 4, core: 2. Of those that a mesh axis runs over, the one named last changes fastest.
Arguments:
- queries: bfloat16 [512, 8192], P('expert', 'tensor'), may hold values from -8 to 8
- keys_values: bfloat16 [4, 4, 1152, 256], P('expert'), may hold values from -6 to 6
- prefix_len: int32 [4], P('expert'), may hold values from 128 to 1024, as said below
- out_proj: bfloat16 [8192, 4096], P('tensor', 'expert'), may hold values from -0.0625 to 0.0625
- residual: bfloat16 [512, 4096], P(('expert', 'tensor')), may hold values from -1.796875 to 1.796875
- norm_gain: float32 [4096], replicated, may hold values from 0.1 to 1.9
- expert_ids: int32 [512, 8], P('expert'), may hold values from 0 to 7, all different within a row; in each aligned block of 16 rows (0 to 15, 16 to 31, ...) at most 16 rows name the same one
- route_weights: bfloat16 [512, 8], P('expert'), may hold values from 0.19921875 to 1
- w_gate: bfloat16 [32, 4096, 384], P(('expert', 'tensor')), may hold values from -0.09375 to 0.09375
- w_up: bfloat16 [32, 4096, 384], P(('expert', 'tensor')), may hold values from -0.09375 to 0.09375
- w_down: bfloat16 [32, 384, 4096], P(('expert', 'tensor')), may hold values from -0.15625 to 0.15625
Outputs:
- layer_out: bfloat16 [512, 4096], P(('expert', 'tensor'))
Inputs may be any that keep to these rules, and one draw needn't show every extreme that they name: `expert_ids`: in the rows of one device (aligned blocks of 16 rows) no expert is named by more than 16 rows, a bound that some block reaches; a row names 8 different experts. `prefix_len`: some sequence has all 1024 slots live.
All inputs are finite; a program needn't handle non-finite values.
Results may differ from a plain program's by a relative error of at most 0.035.
Values may be sent and summed in bfloat16 or wider, within the bound.
A program may use at most 128 MiB of HBM per device.

v0:
```python
import math

import jax
import jax.numpy as jnp
from jax import lax
from jax.sharding import PartitionSpec as P

HEADS = 64
KVH = 4
HD = 128
TOPK = 8
HSPLIT = 4
TOK_DEV = 16
PREFIX = 1024


def norm_rows(hidden_state, norm_gain):
    values = hidden_state.astype(jnp.float32)
    factor = lax.rsqrt(jnp.mean(values * values, axis=-1, keepdims=True) + 1e-06)
    return (values * factor * norm_gain[None, :]).astype(jnp.bfloat16)


def route_tables(expert_ids, route_weights, experts, most_rows):
    total_rows = expert_ids.shape[0]
    named_mask = expert_ids[:, :, None] == jnp.arange(experts, dtype=jnp.int32)[None, None, :]
    hit_table = jnp.sum(named_mask.astype(jnp.int32), axis=1)
    weight_table = jnp.sum(
        jnp.where(named_mask, route_weights[:, :, None].astype(jnp.float32), 0.0), axis=1
    )
    grouped = hit_table.reshape(total_rows // TOK_DEV, TOK_DEV, experts)
    rank_table = (jnp.cumsum(grouped, axis=1) - grouped).reshape(total_rows, experts)
    share_index = (jnp.arange(total_rows, dtype=jnp.int32) // TOK_DEV)[:, None]
    position_table = share_index * most_rows + rank_table
    return (hit_table, weight_table, rank_table, position_table)


def pick_slot(table, expert_count, slot_count, slot_index):
    shaped = table.reshape(table.shape[0], expert_count, slot_count)
    return lax.dynamic_index_in_dim(shaped, slot_index, 2, keepdims=False)


def shards(
    queries,
    keys_values,
    prefix_len,
    out_proj,
    residual,
    norm_gain,
    expert_ids,
    route_weights,
    w_gate,
    w_up,
    w_down,
):
    tensor_count = lax.axis_size("tensor")
    expert_count = lax.axis_size("expert")
    tensor_index = lax.axis_index("tensor")
    step_rows = queries.shape[0]
    per_device = queries.shape[1] // HD
    group_size = HEADS // KVH
    kv_index = tensor_index * per_device // group_size
    cached = lax.dynamic_index_in_dim(keys_values[0], kv_index, 0, keepdims=False)
    key_rows = cached[:, :HD]
    value_rows = cached[:, HD:]
    context = cached.shape[0]
    query_rows = queries.reshape(step_rows, per_device, HD)
    scores = jnp.einsum(
        "nhd,cd->hnc", query_rows, key_rows, preferred_element_type=jnp.float32
    ) / math.sqrt(HD)
    columns = jnp.arange(context, dtype=jnp.int32)[None, :]
    positions = jnp.arange(step_rows, dtype=jnp.int32)[:, None]
    visible = ((columns < prefix_len[0]) | (columns >= PREFIX) & (columns - PREFIX <= positions))[
        None
    ]
    highest = jnp.max(jnp.where(visible, scores, -1e30), axis=-1, keepdims=True)
    weights = jnp.exp(jnp.where(visible, scores - highest, -1e30))
    summed = jnp.sum(weights, axis=-1)
    blended = jnp.einsum(
        "hnc,cd->nhd", weights.astype(jnp.bfloat16), value_rows, preferred_element_type=jnp.float32
    )
    attended = (
        (blended / jnp.transpose(summed)[:, :, None])
        .astype(jnp.bfloat16)
        .reshape(step_rows, per_device * HD)
    )
    head_part = jnp.dot(
        attended,
        lax.all_gather(out_proj, "expert", axis=1, tiled=True),
        preferred_element_type=jnp.float32,
    )
    slot_count = tensor_count // HSPLIT
    experts = expert_count * slot_count
    most_rows = min(TOK_DEV, max(2, TOK_DEV * TOPK // experts + 1))
    capacity = tensor_count * most_rows
    slot_index = tensor_index // HSPLIT
    start_row = tensor_index * TOK_DEV
    hit_table, weight_table, rank_table, position_table = route_tables(
        expert_ids, route_weights, experts, most_rows
    )
    hit_slot = pick_slot(hit_table, expert_count, slot_count, slot_index)
    weight_slot = pick_slot(weight_table, expert_count, slot_count, slot_index)
    position_slot = pick_slot(position_table, expert_count, slot_count, slot_index)
    slot_match = (hit_slot[:, :, None] == 1) & (
        position_slot[:, :, None] == jnp.arange(capacity, dtype=jnp.int32)[None, None, :]
    )
    head_sum = lax.psum(head_part.astype(jnp.bfloat16), "tensor").astype(jnp.float32)
    residual_full = lax.all_gather(residual, "tensor", axis=0, tiled=True)
    state_full = (residual_full.astype(jnp.float32) + head_sum).astype(jnp.bfloat16)
    hidden_state = lax.dynamic_slice_in_dim(state_full, start_row, TOK_DEV, 0)
    normed_full = norm_rows(state_full, norm_gain)
    source_rows = jnp.sum(
        jnp.where(slot_match, jnp.arange(step_rows, dtype=jnp.int32)[:, None, None], 0), axis=0
    )
    filled = jnp.any(slot_match, axis=0)
    outgoing = jnp.where(
        filled[:, :, None], jnp.take(normed_full, source_rows, axis=0), jnp.zeros((), jnp.bfloat16)
    )
    arrived_rows = lax.all_to_all(outgoing, "expert", split_axis=0, concat_axis=0, tiled=True)
    flat_rows = arrived_rows.reshape(-1, arrived_rows.shape[-1])
    gate_val = jnp.dot(flat_rows, w_gate[0], preferred_element_type=jnp.float32)
    up_val = jnp.dot(flat_rows, w_up[0], preferred_element_type=jnp.float32)
    inner = (jax.nn.silu(gate_val) * up_val).astype(jnp.bfloat16)
    result = jnp.dot(inner, w_down[0], preferred_element_type=jnp.float32).astype(jnp.bfloat16)
    computed = result.reshape(arrived_rows.shape)
    returned = lax.all_to_all(computed, "expert", split_axis=0, concat_axis=0, tiled=True)
    combine_weights = jnp.where(slot_match, weight_slot[:, :, None], 0.0).astype(jnp.bfloat16)
    expert_part = jnp.einsum(
        "njc,jcd->nd", combine_weights, returned, preferred_element_type=jnp.float32
    )
    expert_share = lax.psum_scatter(
        expert_part.astype(jnp.bfloat16), "tensor", scatter_dimension=0, tiled=True
    ).astype(jnp.float32)
    return (hidden_state.astype(jnp.float32) + expert_share).astype(jnp.bfloat16)


def solution(mesh):
    return jax.shard_map(
        shards,
        mesh=mesh,
        in_specs=(
            P("expert", "tensor"),
            P("expert", None, None, None),
            P("expert"),
            P("tensor", "expert"),
            P(("expert", "tensor"), None),
            P(),
            P("expert", None),
            P("expert", None),
            P(("expert", "tensor"), None, None),
            P(("expert", "tensor"), None, None),
            P(("expert", "tensor"), None, None),
        ),
        out_specs=P(("expert", "tensor"), None),
        check_vma=False,
    )
```

profile of v0, /device:TPU:0, one launch (start us, length us, event | category | flops | bytes accessed | tf_op | source)
XLA Modules:
  0.0 359.5 jit_solution(12043747940668669427)
XLA Ops:
  6.5 0.7 all-gather.5.cloned.1.call-update
  7.3 0.7 all-gather.3.cloned.1.call-update
  8.8 0.7 convert_reduce_fusion
  9.5 0.1 copy.34
  9.7 0.7 fusion.55
  10.3 0.1 copy.35
  10.5 1.1 dynamic-slice_bitcast_fusion
  11.6 0.8 copy-done.3
  12.4 3.9 %convolution_multiply_fusion = f32[1152,128,8]{1,0,2:T(8,128)} fusion(bf16[1152,256]{1,0:T(8,128)(2,1)S(1)} %dynamic-slice_bitcast_fusion, bf16[128,1024]{1,0:T(8,128)(2,1)} %param.11), kind=kOutput, calls=%fused_computation.10 | convolution fusion | flops 303169536 | bytes 5275648 | tf_op jit(solution)/shard_map/nhd,cd->hnc/dot_general | solution.py:67
  16.4 0.8 select_reduce_fusion.1
  17.2 1.0 fusion.31
  18.2 7.2 %exponential_reduce_fusion = f32[8,128]{1,0:T(8,128)} fusion(f32[1152,128,8]{1,0,2:T(8,128)} %convolution_multiply_fusion, pred[128,1152]{0,1:T(8,128)(4,1)S(1)} %fusion.31), kind=kOutput, calls=%fused_computation.12 | output fusion | flops 4719743 | bytes 4870144 | tf_op jit(solution)/shard_map/sub | solution.py:76
  25.5 5.5 %fusion.27 = bf16[128,8,128]{0,2,1:T(8,128)(2,1)S(1)} fusion(bf16[1152,256]{1,0:T(8,128)(2,1)} %copy-done.3, f32[128,8]{0,1:T(8,128)} %bitcast.95, f32[1152,128,8]{1,0,2:T(8,128)} %convolution_multiply_fusion, pred[128,1152]{0,1:T(8,128)(4,1)S(1)} %fusion.31), kind=kOutput, calls=%fused_computation.33 | convolution fusion | flops 306972800 | bytes 10293248 | tf_op jit(solution)/shard_map/hnc,cd->nhd/dot_general | solution.py:78
  31.0 68.5 %all-gather.5.cloned.1.call-done = bf16[1024,4096]{1,0:T(8,128)(2,1)} async-done(((bf16[1024,1024]{1,0:T(8,128)(2,1)}), bf16[1024,4096]{1,0:T(8,128)(2,1)}) %all-gather.5.cloned.1.call-update) | async-done | bytes 8388624 | tf_op jit(solution)/shard_map/all_gather | solution.py:88
  99.6 5.7 %convolution_convert_fusion.1 = bf16[128,4096]{1,0:T(8,128)(2,1)} fusion(bf16[128,1024]{0,1:T(8,128)(2,1)S(1)} %bitcast.84, bf16[1024,4096]{1,0:T(8,128)(2,1)} %all-gather.5.cloned.1.call-done), kind=kOutput, calls=%fused_computation.5 | convolution fusion | flops 1074266112 | bytes 9699328 | tf_op jit(solution)/shard_map/dot_general | solution.py:86
  105.4 0.2 fusion.36
  105.6 17.7 %all-gather.3.cloned.1.call-done = bf16[128,4096]{1,0:T(8,128)(2,1)} async-done(((bf16[16,4096]{1,0:T(8,128)(2,1)}), bf16[128,4096]{1,0:T(8,128)(2,1)}) %all-gather.3.cloned.1.call-update) | async-done | bytes 1048592 | tf_op jit(solution)/shard_map/all_gather | solution.py:107
  123.3 60.9 %all-reduce.2.cloned.1.call-done = bf16[128,4096]{1,0:T(8,128)(2,1)} async-done(((bf16[128,4096]{1,0:T(8,128)(2,1)}), bf16[128,4096]{1,0:T(8,128)(2,1)}) %all-reduce.2.cloned.1.call-update) | async-done | bytes 1048592 | tf_op jit(solution)/shard_map/psum | solution.py:106
  184.2 2.0 fusion.16
  186.2 1.1 copy-done.1
  187.2 1.3 fusion.18
  188.6 9.9 %gather_fusion = bf16[512,4096]{1,0:T(8,128)(2,1)} fusion(bf16[128,4096]{1,0:T(8,128)(2,1)} %fusion.18, s32[1024]{0:T(1024)S(1)} %pad_clamp_fusion), kind=kCustom, calls=%fused_computation | custom fusion | bytes 8390656 | tf_op jit(solution)/shard_map/jit(_take)/gather | solution.py:116
  198.5 2.6 select_select_fusion
  201.1 49.7 %all_to_all.10 = bf16[4,128,4096]{2,1,0:T(8,128)(2,1)S(1)} all-to-all(bf16[4,128,4096]{2,1,0:T(8,128)(2,1)S(1)} %select_select_fusion), channel_id=1, replica_groups=mesh['expert'=4,'tensor'=8] {'expert'}, dimensions={0} | all-to-all | bytes 8388608 | tf_op jit(solution)/shard_map/all_to_all | solution.py:118
  250.8 2.0 copy-done.2
  252.7 3.2 fusion.11
  256.0 9.7 %convolution_convert_fusion = bf16[512,4096]{1,0:T(8,128)(2,1)} fusion(bf16[1,384,4096]{2,1,0:T(8,128)(2,1)S(1)} %copy-done, bf16[512,4096]{1,0:T(8,128)(2,1)} %bitcast.83, bf16[1,4096,384]{2,1,0:T(8,128)(2,1)} %param.20, f32[512,384]{1,0:T(8,128)} %fusion.11), kind=kOutput, calls=%fused_computation.2 | convolution fusion | flops 3224502272 | bytes 15466496 | tf_op jit(solution)/shard_map/dot_general | solution.py:123
  265.7 5.0 %all-to-all-start.1 = ((bf16[4,128,4096]{2,1,0:T(8,128)(2,1)}), bf16[4,128,4096]{2,1,0:T(8,128)(2,1)}, u32[]{:S(2)}, u32[]{:S(2)}) async-start(bf16[4,128,4096]{2,1,0:T(8,128)(2,1)} %bitcast.81), calls=%async_computation.1 | async-start | bytes 8388608 | tf_op jit(solution)/shard_map/all_to_all | solution.py:125
  270.8 44.0 %all-to-all-done.1 = bf16[4,128,4096]{2,1,0:T(8,128)(2,1)} async-done(((bf16[4,128,4096]{2,1,0:T(8,128)(2,1)}), bf16[4,128,4096]{2,1,0:T(8,128)(2,1)}, u32[]{:S(2)}, u32[]{:S(2)}) %all-to-all-start.1) | async-done | bytes 4194336 | tf_op jit(solution)/shard_map/all_to_all | solution.py:125
  314.8 4.1 %fusion.1 = bf16[128,4096]{1,0:T(8,128)(2,1)} fusion(bf16[4,128,4096]{2,1,0:T(8,128)(2,1)} %all-to-all-done.1, f32[128,4]{0,1:T(4,128)S(1)} %bitcast.88, s32[128,4]{0,1:T(4,128)S(1)} %bitcast.87, pred[128,4]{0,1:T(4,128)(4,1)S(1)} %bitcast.93), kind=kOutput, calls=%fused_computation.4 | convolution fusion | flops 537591808 | bytes 5247488 | tf_op jit(solution)/shard_map/njc,jcd->nd/dot_general | solution.py:127
  318.9 32.4 %reduce-scatter.2.cloned.1.call-done = bf16[16,4096]{1,0:T(8,128)(2,1)} async-done(((bf16[128,4096]{1,0:T(8,128)(2,1)}), bf16[16,4096]{1,0:T(8,128)(2,1)}) %reduce-scatter.2.cloned.1.call-update) | async-done | bytes 131088 | tf_op jit(solution)/shard_map/reduce_scatter | solution.py:130
  351.3 1.7 add_convert_fusion.1
  (44 shorter events, 0.5 us)
Async XLA Ops:
  6.5 249.4 %copy-start = (bf16[1,384,4096]{2,1,0:T(8,128)(2,1)S(1)}, bf16[1,384,4096]{2,1,0:T(8,128)(2,1)}, u32[]{:S(2)}) copy-start(bf16[1,384,4096]{2,1,0:T(8,128)(2,1)} %param.21) | copy-start | bytes 9437188
  6.5 93.0 %all-gather.5.cloned.1.call-start = ((), (), s32[]{:S(2)}) async-start(), calls=%async_computation.4 | async-start | bytes 10485760 | tf_op jit(solution)/shard_map/all_gather | solution.py:88
  7.3 116.0 %all-gather.3.cloned.1.call-start = ((), (), s32[]{:S(2)}) async-start(), calls=%async_computation.3 | async-start | bytes 1179648 | tf_op jit(solution)/shard_map/all_gather | solution.py:107
  8.0 176.2 %all-reduce.2.cloned.1.call-start = ((), (), s32[]{:S(2)}) async-start(), calls=%async_computation.5 | async-start | bytes 2097152 | tf_op jit(solution)/shard_map/psum | solution.py:106
  11.6 0.8 copy-start.3
  16.3 0.9 copy-start.4
  16.4 0.8 copy-start.6
  99.6 5.8 %copy-start.8 = (s32[4,128]{1,0:T(4,128)S(1)}, s32[4,128]{1,0:T(4,128)}, u32[]{:S(2)}) copy-start(s32[4,128]{1,0:T(4,128)} %select_reduce_fusion.1) | copy-start | bytes 6148
  99.6 5.8 %copy-start.5 = (s32[128,4,1]{0,2,1:T(1,128)S(1)}, s32[128,4,1]{0,2,1:T(1,128)}, u32[]{:S(2)}) copy-start(s32[128,4,1]{0,2,1:T(1,128)} %copy-done.4) | copy-start | bytes 6148
  99.6 5.8 %copy-start.7 = (pred[128,4,1]{0,1,2:T(4,128)(4,1)S(1)}, pred[128,4,1]{0,1,2:T(4,128)(4,1)}, u32[]{:S(2)}) copy-start(pred[128,4,1]{0,1,2:T(4,128)(4,1)} %copy-done.6) | copy-start | bytes 1540
  105.3 81.9 %copy-start.9 = (f32[4096]{0:T(1024)S(1)}, f32[4096]{0:T(1024)}, u32[]{:S(2)}) copy-start(f32[4096]{0:T(1024)} %param.16) | copy-start | bytes 49156
  186.2 1.1 copy-start.1
  201.1 51.7 %copy-start.12 = (bf16[1,4096,384]{2,1,0:T(8,128)(2,1)S(1)}, bf16[1,4096,384]{2,1,0:T(8,128)(2,1)}, u32[]{:S(2)}) copy-start(bf16[1,4096,384]{2,1,0:T(8,128)(2,1)} %param.19) | copy-start | bytes 9437188
  250.8 2.0 copy-start.2
  265.7 5.0 %copy-start.11 = (bf16[128,8]{0,1:T(8,128)(2,1)S(1)}, bf16[128,8]{0,1:T(8,128)(2,1)}, u32[]{:S(2)}) copy-start(bf16[128,8]{0,1:T(8,128)(2,1)} %param.18) | copy-start | bytes 6148
  265.7 5.1 %copy-start.10 = (s32[128,8]{0,1:T(8,128)S(1)}, s32[128,8]{0,1:T(8,128)}, u32[]{:S(2)}) copy-start(s32[128,8]{0,1:T(8,128)} %param.17) | copy-start | bytes 12292
  265.7 49.1 %all-to-all-start.1 = ((bf16[4,128,4096]{2,1,0:T(8,128)(2,1)}), bf16[4,128,4096]{2,1,0:T(8,128)(2,1)}, u32[]{:S(2)}, u32[]{:S(2)}) async-start(bf16[4,128,4096]{2,1,0:T(8,128)(2,1)} %bitcast.81), calls=%async_computation.1 | async-start | bytes 8388608 | tf_op jit(solution)/shard_map/all_to_all | solution.py:125
  270.7 80.6 %reduce-scatter.2.cloned.1.call-start = ((), (), s32[]{:S(2)}) async-start(), calls=%async_computation.6 | async-start | bytes 1179648 | tf_op jit(solution)/shard_map/reduce_scatter | solution.py:130
Sparse Core Ops, SparseCore 0:
  9.2 90.2 all-gather.4
  101.1 22.0 all-gather.2
  125.6 58.4 all-reduce.1
  319.0 32.2 reduce-scatter.1
where the time goes:
time: 360 us
  waiting for transfers between devices  225 us (62%)
  blocking collectives  49.7 us (14%)
  matrix products  32.2 us (9%)
  other arithmetic  18.3 us (5%)
  local copies, waits for them, and re-layouts  15.3 us (4%)
  between operations  14.1 us (4%)
  starting transfers between devices  5.09 us (1%)
    all_gather x1, waiting for transfers between devices, shards(): lax.all_gather(out_proj, 'expert', axis=1, tiled=True)  68.5 us
    psum x1, waiting for transfers between devices, shards(): lax.psum(head_part.astype(jnp.bfloat16), 'tensor').astype(jnp.float32)  60.9 us
    all_to_all x1, blocking collectives, shards(): lax.all_to_all(outgoing, 'expert', split_axis=0, concat_axis=0, tiled=True)  49.7 us
    all_to_all x1, waiting for transfers between devices, shards(): lax.all_to_all(computed, 'expert', split_axis=0, concat_axis=0, tiled=True)  44 us
    reduce_scatter x1, waiting for transfers between devices, shards(): lax.psum_scatter(expert_part.astype(jnp.bfloat16), 'tensor', scatter_dime...  32.4 us
    all_gather x1, waiting for transfers between devices, shards(): residual_full = lax.all_gather(residual, 'tensor', axis=0, tiled=True)  17.7 us
    gather x1, local copies, waits for them, and re-layouts, shards(): jnp.take(normed_full, source_rows, axis=0)  9.92 us
    dot_general x1, matrix products, shards(): jnp.dot(inner, w_down[0], preferred_element_type=jnp.float32)  9.71 us
  transfers between devices with their start and end apart: 5, of which 5 were waited for; matrix products, arithmetic and copies ran while one was open for 8% of the time, Pallas kernels for 0%

commit v1 on v0

--- a/solution.py
+++ b/solution.py
@@ -133,9 +133,96 @@
     return (hidden_state.astype(jnp.float32) + expert_share).astype(jnp.bfloat16)
 
 
+def weight_columns(expert_ids, route_weights, experts):
+    named_mask = expert_ids[:, :, None] == jnp.arange(experts, dtype=jnp.int32)[None, None, :]
+    return jnp.sum(
+        jnp.where(named_mask, route_weights[:, :, None].astype(jnp.float32), 0.0), axis=1
+    )
+
+
+def attend(queries, keys_values, prefix_len):
+    tensor_index = lax.axis_index("tensor")
+    step_rows = queries.shape[0]
+    per_device = queries.shape[1] // HD
+    kv_index = tensor_index * per_device // (HEADS // KVH)
+    cached = lax.dynamic_index_in_dim(keys_values[0], kv_index, 0, keepdims=False)
+    key_rows = cached[:, :HD]
+    value_rows = cached[:, HD:]
+    context = cached.shape[0]
+    query_rows = queries.reshape(step_rows, per_device, HD)
+    scores = jnp.einsum(
+        "nhd,cd->hnc", query_rows, key_rows, preferred_element_type=jnp.float32
+    ) / math.sqrt(HD)
+    columns = jnp.arange(context, dtype=jnp.int32)[None, :]
+    positions = jnp.arange(step_rows, dtype=jnp.int32)[:, None]
+    visible = ((columns < prefix_len[0]) | (columns >= PREFIX) & (columns - PREFIX <= positions))[
+        None
+    ]
+    highest = jnp.max(jnp.where(visible, scores, -1e30), axis=-1, keepdims=True)
+    weights = jnp.exp(jnp.where(visible, scores - highest, -1e30))
+    summed = jnp.sum(weights, axis=-1)
+    blended = jnp.einsum(
+        "hnc,cd->nhd", weights.astype(jnp.bfloat16), value_rows, preferred_element_type=jnp.float32
+    )
+    return (
+        (blended / jnp.transpose(summed)[:, :, None])
+        .astype(jnp.bfloat16)
+        .reshape(step_rows, per_device * HD)
+    )
+
+
+def dense_shards(
+    queries,
+    keys_values,
+    prefix_len,
+    out_proj,
+    residual,
+    norm_gain,
+    expert_ids,
+    route_weights,
+    w_gate,
+    w_up,
+    w_down,
+):
+    tensor_count = lax.axis_size("tensor")
+    expert_count = lax.axis_size("expert")
+    slot_count = tensor_count // HSPLIT
+    experts = expert_count * slot_count
+    own_expert = lax.axis_index("expert") * slot_count + lax.axis_index("tensor") // HSPLIT
+    weight_table = weight_columns(expert_ids, route_weights, experts).astype(jnp.bfloat16)
+    weight_all = lax.all_gather(weight_table, "expert", axis=0, tiled=True)
+    own_weight = lax.dynamic_slice_in_dim(weight_all, own_expert, 1, 1).astype(jnp.float32)
+    attended = attend(queries, keys_values, prefix_len)
+    attended_all = lax.all_gather(attended, "expert", axis=0, tiled=True)
+    head_part = jnp.dot(attended_all, out_proj, preferred_element_type=jnp.float32)
+    head_part = head_part.astype(jnp.bfloat16).reshape(
+        expert_count, tensor_count, TOK_DEV, out_proj.shape[1]
+    )
+    head_sum = lax.psum_scatter(head_part, "tensor", scatter_dimension=1, tiled=True)
+    head_sum = lax.all_to_all(
+        head_sum.reshape(expert_count, TOK_DEV, -1), "expert", split_axis=0, concat_axis=2, tiled=True
+    )[0]
+    hidden_state = (residual.astype(jnp.float32) + head_sum.astype(jnp.float32)).astype(
+        jnp.bfloat16
+    )
+    normed = norm_rows(hidden_state, norm_gain)
+    normed_all = lax.all_gather(normed, ("expert", "tensor"), axis=0, tiled=True)
+    gate_val = jnp.dot(normed_all, w_gate[0], preferred_element_type=jnp.float32)
+    up_val = jnp.dot(normed_all, w_up[0], preferred_element_type=jnp.float32)
+    inner = (jax.nn.silu(gate_val) * up_val).astype(jnp.bfloat16)
+    result = jnp.dot(inner, w_down[0], preferred_element_type=jnp.float32)
+    part = (result * own_weight).astype(jnp.bfloat16)
+    expert_share = lax.psum_scatter(part, ("expert", "tensor"), scatter_dimension=0, tiled=True)
+    return (hidden_state.astype(jnp.float32) + expert_share.astype(jnp.float32)).astype(
+        jnp.bfloat16
+    )
+
+
 def solution(mesh):
+    experts = mesh.shape["expert"] * mesh.shape["tensor"] // HSPLIT
+    dense = experts == TOPK
     return jax.shard_map(
-        shards,
+        dense_shards if dense else shards,
         mesh=mesh,
         in_specs=(
             P("expert", "tensor"),

time: 360 us -> 350 us (0.972)
  waiting for transfers between devices: 225 us -> 281 us
  blocking collectives: 49.7 us -> 15.9 us
  other arithmetic: 18.3 us -> 5.33 us
  local copies, waits for them, and re-layouts: 15.3 us -> 4.56 us
  starting transfers between devices: 5.09 us -> 0.13 us
  matrix products: 32.2 us -> 28.3 us
    reduce_scatter x1, waiting for transfers between devices: 32.4 us -> 141 us  [dense_shards(): lax.psum_scatter(part, ('expert', 'tensor'), scatter_dimension=0, tiled=T...]
    psum x1 -> x0, waiting for transfers between devices: 60.9 us -> none  [shards(): lax.psum(head_part.astype(jnp.bfloat16), 'tensor').astype(jnp.float32)]
    unnamed x4 -> x5, waiting for transfers between devices: 1.44 us -> 58.4 us
    all_to_all x1 -> x0, waiting for transfers between devices: 44 us -> none  [shards(): lax.all_to_all(computed, 'expert', split_axis=0, concat_axis=0, tiled=True)]
    all_to_all x1, blocking collectives: 49.7 us -> 8.45 us  [dense_shards(): lax.all_to_all(head_sum.reshape(expert_count, TOK_DEV, -1), 'expert', spl...]
    gather x1 -> x0, local copies, waits for them, and re-layouts: 9.92 us -> none  [shards(): jnp.take(normed_full, source_rows, axis=0)]
    all_gather x0 -> x1, blocking collectives: none -> 7.47 us  [dense_shards(): weight_all = lax.all_gather(weight_table, 'expert', axis=0, tiled=True)]
    sub x2, other arithmetic: 7.24 us -> 1.71 us  [the longest x1 1.71 us: attend(): weights = jnp.exp(jnp.where(visible, scores - highest, -1e+30))]
  transfers between devices with their start and end apart: 5 -> 4, of which waited for: 5 -> 4; matrix products, arithmetic and copies ran while one was open for 8% -> 0% of each run, Pallas kernels for 0% -> 0%
where the time goes in v1:
time: 350 us; the launch traced here: 349 us
  waiting for transfers between devices  281 us (80%)
  matrix products  28.3 us (8%)
  blocking collectives  15.9 us (5%)
  between operations  14.1 us (4%)
  other arithmetic  5.33 us (2%)
  local copies, waits for them, and re-layouts  4.56 us (1%)
    reduce_scatter x1, waiting for transfers between devices, dense_shards(): lax.psum_scatter(part, ('expert', 'tensor'), scatter_dimension=0, tiled=T...  141 us
    unnamed x5, waiting for transfers between devices  58.4 us
    all_gather x1, waiting for transfers between devices, dense_shards(): lax.all_gather(normed, ('expert', 'tensor'), axis=0, tiled=True)  52.2 us
    all_gather x1, waiting for transfers between devices, dense_shards(): attended_all = lax.all_gather(attended, 'expert', axis=0, tiled=True)  29.3 us
    dot_general x1, matrix products, dense_shards(): result = jnp.dot(inner, w_down[0], preferred_element_type=jnp.float32)  9.73 us
    all_to_all x1, blocking collectives, dense_shards(): lax.all_to_all(head_sum.reshape(expert_count, TOK_DEV, -1), 'expert', spl...  8.45 us
    all_gather x1, blocking collectives, dense_shards(): weight_all = lax.all_gather(weight_table, 'expert', axis=0, tiled=True)  7.47 us
  transfers between devices with their start and end apart: 4, of which 4 were waited for; matrix products, arithmetic and copies ran while one was open for 0% of the time, Pallas kernels for 0%

profile of v1, /device:TPU:0, one launch (start us, length us, event | category | flops | bytes accessed | tf_op | source)
XLA Modules:
  0.0 349.5 jit_solution(16239609666158277767)
XLA Ops:
  7.4 1.2 dynamic-slice_bitcast_fusion
  8.6 0.0 copy-start.2
  8.6 0.8 copy-done.2
  9.4 1.7 convolution_multiply_fusion
  11.2 1.0 fusion.27
  12.2 1.7 exponential_reduce_fusion
  13.9 0.0 copy-done.1
  13.9 6.2 %fusion.23 = bf16[128,8,128]{0,2,1:T(8,128)(2,1)} fusion(bf16[1152,256]{1,0:T(8,128)(2,1)} %copy-done.2, f32[128,8]{0,1:T(8,128)S(1)} %bitcast.80, f32[1152,128,8]{1,0,2:T(8,128)} %copy-done.1, pred[128,1152]{0,1:T(8,128)(4,1)S(1)} %fusion.27), kind=kOutput, calls=%fused_computation.23 | convolution fusion | flops 306972800 | bytes 10293248 | tf_op jit(solution)/shard_map/hnc,cd->nhd/dot_general | solution.py:164
  20.2 0.0 copy-start.5
  20.2 0.0 all-gather.3.cloned.1.call-update
  20.2 0.0 all-reduce.3.cloned.1.call-start
  20.3 29.3 %all-gather.3.cloned.1.call-done = bf16[512,1024]{0,1:T(8,128)(2,1)} async-done(((bf16[128,1024]{0,1:T(8,128)(2,1)}), bf16[512,1024]{0,1:T(8,128)(2,1)}) %all-gather.3.cloned.1.call-update) | async-done | bytes 1048592 | tf_op jit(solution)/shard_map/all_gather | solution.py:196
  49.6 4.2 %convolution_convert_fusion = bf16[512,1024]{1,0:T(8,128)(2,1)} fusion(bf16[512,1024]{0,1:T(8,128)(2,1)} %all-gather.3.cloned.1.call-done, bf16[1024,1024]{1,0:T(8,128)(2,1)} %param.14), kind=kOutput, calls=%fused_computation.18 | convolution fusion | flops 1074266112 | bytes 4194304 | tf_op jit(solution)/shard_map/dot_general | solution.py:197
  53.8 0.0 all-reduce.3.cloned.1.call-update
  53.8 0.0 all-gather.5.cloned.1.call-start
  53.9 0.6 dynamic-slice.1
  54.5 58.3 %all-reduce.3.cloned.1.call-done = bf16[4,8,16,1024]{3,2,1,0:T(8,128)(2,1)} async-done(((bf16[4,8,16,1024]{3,2,1,0:T(8,128)(2,1)}), bf16[4,8,16,1024]{3,2,1,0:T(8,128)(2,1)}) %all-reduce.3.cloned.1.call-update) | async-done | bytes 1048592
  112.8 1.6 dynamic-slice_bitcast_fusion.1
  114.3 8.4 %all_to_all.4 = bf16[4,16,1024]{2,1,0:T(8,128)(2,1)S(1)} all-to-all(bf16[4,16,1024]{2,1,0:T(8,128)(2,1)S(1)} %dynamic-slice_bitcast_fusion.1), channel_id=1, replica_groups=mesh['expert'=4,'tensor'=8] {'expert'}, dimensions={0} | all-to-all | bytes 262144 | tf_op jit(solution)/shard_map/all_to_all | solution.py:202
  122.8 0.2 copy.33
  123.0 0.2 copy.40
  123.2 0.2 fusion.29
  123.3 0.8 fusion.31
  124.1 0.0 all-gather.5.cloned.1.call-update
  124.1 0.0 reduce-scatter.5.cloned.1.call-start
  124.3 7.5 %all_gather.11 = bf16[512,8]{0,1:T(8,128)(2,1)S(1)} all-gather(bf16[128,8]{0,1:T(8,128)(2,1)S(1)} %select_reduce_fusion.1), channel_id=1, replica_groups=mesh['expert'=4,'tensor'=8] {'expert'}, dimensions={0}, use_global_device_ids=true | all-gather | bytes 10240 | tf_op jit(solution)/shard_map/all_gather | solution.py:193
  131.7 52.2 %all-gather.5.cloned.1.call-done = bf16[512,4096]{1,0:T(8,128)(2,1)} async-done(((bf16[16,4096]{1,0:T(8,128)(2,1)}), bf16[512,4096]{1,0:T(8,128)(2,1)}) %all-gather.5.cloned.1.call-update) | async-done | bytes 4194320 | tf_op jit(solution)/shard_map/all_gather | solution.py:209
  183.9 6.4 %fusion.10 = f32[512,384]{1,0:T(8,128)} fusion(bf16[512,4096]{1,0:T(8,128)(2,1)} %all-gather.5.cloned.1.call-done, bf16[1,4096,384]{2,1,0:T(8,128)(2,1)} %param.19), kind=kOutput, calls=%fused_computation.13 | convolution fusion | flops 1610612736 | bytes 8126464 | tf_op jit(solution)/shard_map/dot_general | solution.py:210
  190.3 9.7 %multiply_convert_fusion = bf16[512,4096]{1,0:T(8,128)(2,1)} fusion(f32[512]{0:T(512)S(1)} %bitcast.79, bf16[1,384,4096]{2,1,0:T(8,128)(2,1)S(1)} %copy-done, bf16[512,4096]{1,0:T(8,128)(2,1)} %all-gather.5.cloned.1.call-done, bf16[1,4096,384]{2,1,0:T(8,128)(2,1)} %param.20, f32[512,384]{1,0:T(8,128)} %fusion.10), kind=kOutput, calls=%fused_computation.1 | convolution fusion | flops 3226599424 | bytes 15468544 | tf_op jit(solution)/shard_map/dot_general | solution.py:213
  200.1 0.0 reduce-scatter.5.cloned.1.call-update
  200.1 141.3 %reduce-scatter.5.cloned.1.call-done = bf16[16,4096]{1,0:T(8,128)(2,1)} async-done(((bf16[512,4096]{1,0:T(8,128)(2,1)}), bf16[16,4096]{1,0:T(8,128)(2,1)}) %reduce-scatter.5.cloned.1.call-update) | async-done | bytes 131088 | tf_op jit(solution)/shard_map/reduce_scatter | solution.py:215
  341.4 1.6 fusion.32
  (20 shorter events, 0.1 us)
Async XLA Ops:
  6.5 183.8 %copy-start = (bf16[1,384,4096]{2,1,0:T(8,128)(2,1)S(1)}, bf16[1,384,4096]{2,1,0:T(8,128)(2,1)}, u32[]{:S(2)}) copy-start(bf16[1,384,4096]{2,1,0:T(8,128)(2,1)} %param.21) | copy-start | bytes 9437188
  6.5 43.0 %all-gather.3.cloned.1.call-start = ((), (), s32[]{:S(2)}) async-start(), calls=%async_computation.2 | async-start | bytes 1310720 | tf_op jit(solution)/shard_map/all_gather | solution.py:196
  8.6 0.8 copy-start.2
  11.2 2.8 copy-start.1
  20.2 33.7 %copy-start.7 = (u32[32]{0:T(128)S(1)}, u32[32]{0:T(128)}, u32[]{:S(2)}) copy-start(u32[32]{0:T(128)} %constant.73) | copy-start | bytes 388
  20.2 103.0 %copy-start.3 = (bf16[16,4096]{1,0:T(8,128)(2,1)S(1)}, bf16[16,4096]{1,0:T(8,128)(2,1)}, u32[]{:S(2)}) copy-start(bf16[16,4096]{1,0:T(8,128)(2,1)} %param.15) | copy-start | bytes 393220
  20.2 103.2 %copy-start.4 = (f32[4096]{0:T(1024)S(1)}, f32[4096]{0:T(1024)}, u32[]{:S(2)}) copy-start(f32[4096]{0:T(1024)} %param.16) | copy-start | bytes 49156
  20.2 104.0 %copy-start.6 = (bf16[128,8]{0,1:T(8,128)(2,1)S(1)}, bf16[128,8]{0,1:T(8,128)(2,1)}, u32[]{:S(2)}) copy-start(bf16[128,8]{0,1:T(8,128)(2,1)} %param.18) | copy-start | bytes 6148
  20.2 104.0 %copy-start.5 = (s32[128,8]{0,1:T(8,128)S(1)}, s32[128,8]{0,1:T(8,128)}, u32[]{:S(2)}) copy-start(s32[128,8]{0,1:T(8,128)} %param.17) | copy-start | bytes 12292
  20.2 92.5 %all-reduce.3.cloned.1.call-start = ((), (), s32[]{:S(2)}) async-start(), calls=%async_computation.5 | async-start | bytes 2097152
  53.8 130.1 %all-gather.5.cloned.1.call-start = ((), (), s32[]{:S(2)}) async-start(), calls=%async_computation.3 | async-start | bytes 4325376 | tf_op jit(solution)/shard_map/all_gather | solution.py:209
  124.1 217.2 %reduce-scatter.5.cloned.1.call-start = ((), (), s32[]{:S(2)}) async-start(), calls=%async_computation.4 | async-start | bytes 4325376 | tf_op jit(solution)/shard_map/reduce_scatter | solution.py:215
Sparse Core Ops, SparseCore 0:
  20.3 29.1 all-gather.2
  53.9 58.7 all-reduce.2
  124.2 59.6 all-gather.4
  200.2 141.1 reduce-scatter.4

commit v2 on v1

--- a/solution.py
+++ b/solution.py
@@ -3,6 +3,8 @@
 import jax
 import jax.numpy as jnp
 from jax import lax
+from jax.experimental import pallas as pl
+from jax.experimental.pallas import tpu as pltpu
 from jax.sharding import PartitionSpec as P
 
 HEADS = 64
@@ -171,6 +173,328 @@
     )
 
 
+LANES = 128
+COPIES = 128
+
+
+def layer_kernel(
+    attended,
+    proj_hbm,
+    residual,
+    gain,
+    route,
+    gate_hbm,
+    up_hbm,
+    down_hbm,
+    out,
+    proj,
+    gate,
+    up,
+    down,
+    seen,
+    heads,
+    heads_sib,
+    head_sum,
+    heads_z,
+    col_out,
+    col_in,
+    hidden,
+    rows,
+    part,
+    part_sib,
+    diag_y,
+    diag_x,
+    part_x,
+    part_y,
+    z_out,
+    z_in,
+    send_sem,
+    recv_sem,
+    load_sem,
+):
+    width = residual.shape[1]
+    half = width // 2
+    e = lax.axis_index("expert")
+    t = lax.axis_index("tensor")
+    x, y, z, c = e % 2, e // 2, t // 2, t % 2
+    flat = [
+        e,
+        y * 2 + (1 - x),
+        (1 - y) * 2 + x,
+        (1 - y) * 2 + (1 - x),
+    ]
+    line = [(z + k) % 4 for k in range(4)]
+    to_x, to_y, to_diag = (flat[1], t), (flat[2], t), (flat[3], t)
+    to_sib = (e, z * 2 + (1 - c))
+    to_z = [None] + [(e, line[k] * 2 + c) for k in range(1, 4)]
+
+    loads = []
+    for index, (source, target) in enumerate(
+        ((proj_hbm, proj), (gate_hbm, gate), (up_hbm, up), (down_hbm, down))
+    ):
+        loads.append(pltpu.make_async_copy(source, target, load_sem.at[index]))
+        loads[-1].start()
+
+    barrier = pltpu.get_barrier_semaphore()
+    for partner in (to_x, to_y, to_diag, to_sib, *to_z[1:]):
+        pl.semaphore_signal(
+            barrier, inc=1, device_id=partner, device_id_type=pl.DeviceIdType.MESH
+        )
+    pl.semaphore_wait(barrier, 7)
+
+    sent = []
+
+    def send(source, target, partner):
+        number = len(sent)
+        copy = pltpu.make_async_remote_copy(
+            src_ref=source,
+            dst_ref=target,
+            send_sem=send_sem.at[number],
+            recv_sem=recv_sem.at[number],
+            device_id=partner,
+            device_id_type=pl.DeviceIdType.MESH,
+        )
+        copy.start()
+        sent.append(copy)
+        return copy
+
+    row_half = attended.shape[0] // 2
+    top, low = pl.ds(0, row_half), pl.ds(row_half, row_half)
+    x_top = send(attended.at[top], seen.at[0, top], to_x)
+    y_low = send(attended.at[low], seen.at[1, low], to_y)
+    x_low = send(attended.at[low], seen.at[0, low], to_x)
+    y_top = send(attended.at[top], seen.at[1, top], to_y)
+
+    def project(source, r):
+        @pl.loop(0, proj.shape[1] // 256)
+        def _(tile):
+            columns = pl.ds(pl.multiple_of(tile * 256, 256), 256)
+            value = jnp.dot(source[...], proj[:, columns], preferred_element_type=jnp.float32)
+            heads[r, :, :, :, columns] = value.astype(jnp.bfloat16).reshape(4, 2, TOK_DEV, 256)
+
+        return send(heads.at[r, :, 1 - c], heads_sib.at[r], to_sib)
+
+    def add_cores(r, copy):
+        copy.wait_recv()
+
+        @pl.loop(0, 4)
+        def _(place):
+            head_sum[r, place] = (
+                heads[r, place, c].astype(jnp.float32)
+                + heads_sib[r, place].astype(jnp.float32)
+            ).astype(jnp.bfloat16)
+
+        return [
+            send(head_sum.at[r, line[k]], heads_z.at[r, (4 - k) % 4], to_z[k])
+            for k in (2, 1, 3)
+        ]
+
+    loads[0].wait()
+    sib = [project(attended, 0), None, None, None]
+    x_top.wait_recv()
+    d_top = send(seen.at[0, top], seen.at[2, top], to_y)
+    y_low.wait_recv()
+    d_low = send(seen.at[1, low], seen.at[2, low], to_x)
+    along = [None] * 4
+    x_low.wait_recv()
+    sib[1] = project(seen.at[0], 1)
+    along[0] = add_cores(0, sib[0])
+    y_top.wait_recv()
+    sib[2] = project(seen.at[1], 2)
+    along[1] = add_cores(1, sib[1])
+    d_top.wait_recv()
+    d_low.wait_recv()
+    sib[3] = project(seen.at[2], 3)
+    along[2] = add_cores(2, sib[2])
+    along[3] = add_cores(3, sib[3])
+
+    columns_in = [None] * 4
+    for r in (1, 2, 3, 0):
+        for copy in along[r]:
+            copy.wait_recv()
+        total = head_sum[r, z].astype(jnp.float32)
+        for k in range(1, 4):
+            total = total + heads_z[r, k].astype(jnp.float32)
+        if r:
+            col_out[r] = total.astype(jnp.bfloat16)
+            columns_in[r] = send(col_out.at[r], col_in.at[r], (flat[r], t))
+        else:
+            col_in[0] = total.astype(jnp.bfloat16)
+    quarter = width // 4
+    square = jnp.zeros((TOK_DEV, 1), jnp.float32)
+    for r in range(4):
+        if r:
+            columns_in[r].wait_recv()
+        columns = pl.ds(pl.multiple_of(flat[r] * quarter, quarter), quarter)
+        state = residual[:, columns].astype(jnp.float32) + col_in[r].astype(jnp.float32)
+        state = state.astype(jnp.bfloat16).astype(jnp.float32)
+        hidden[:, columns] = state
+        square = square + jnp.sum(state * state, axis=1, keepdims=True)
+    factor = lax.rsqrt(square / width + 1e-06)
+    own = pl.ds(0, TOK_DEV)
+    rows[0, own, pl.ds(0, width)] = (hidden[...] * factor * gain[...]).astype(jnp.bfloat16)
+    rows[0, own, pl.ds(width, LANES)] = route[...]
+
+    full = rows.shape[2]
+    first, last = pl.ds(0, half), pl.ds(half, full - half)
+
+    def block(r, d):
+        return pl.ds((d * 4 + r) * TOK_DEV, TOK_DEV)
+
+    order = (0, 1, 3, 2)
+    z_rows = [None] + [
+        send(rows.at[0, own], rows.at[(4 - k) % 4, own], to_z[k]) for k in range(1, 4)
+    ]
+    x_rows, y_rows, d_first, d_last = {}, {}, {}, {}
+    other = {k: [] for k in order}
+
+    def spread(k):
+        if k:
+            z_rows[(4 - k) % 4].wait_recv()
+        x_rows[k] = send(rows.at[k, own], rows.at[k, block(1, 0)], to_x)
+        y_rows[k] = send(rows.at[k, own], rows.at[k, block(2, 0)], to_y)
+        other[k].append(send(rows.at[k, own], rows.at[k, block(0, 1)], to_sib))
+
+    def pass_on(k):
+        x_rows[k].wait_recv()
+        d_first[k] = send(
+            rows.at[k, block(1, 0), first], rows.at[k, block(3, 0), first], to_y
+        )
+        other[k].append(send(rows.at[k, block(1, 0)], rows.at[k, block(1, 1)], to_sib))
+        y_rows[k].wait_recv()
+        d_last[k] = send(rows.at[k, block(2, 0), last], rows.at[k, block(3, 0), last], to_x)
+        other[k].append(send(rows.at[k, block(2, 0)], rows.at[k, block(2, 1)], to_sib))
+
+    def complete(k):
+        d_first[k].wait_recv()
+        d_last[k].wait_recv()
+        other[k].append(send(rows.at[k, block(3, 0)], rows.at[k, block(3, 1)], to_sib))
+
+    own_expert = e * 2 + t // HSPLIT
+    part_copies = {}
+
+    def experts(k):
+        for copy in other[k]:
+            copy.wait_recv()
+        values = rows.at[k, :, pl.ds(0, width)]
+        gate_val = jnp.dot(values[...], gate[...], preferred_element_type=jnp.float32)
+        up_val = jnp.dot(values[...], up[...], preferred_element_type=jnp.float32)
+        inner = (gate_val / (1.0 + jnp.exp(-gate_val)) * up_val).astype(jnp.bfloat16)
+        named = lax.broadcasted_iota(jnp.int32, (8 * TOK_DEV, LANES), 1) == own_expert
+        weight = jnp.sum(
+            jnp.where(named, rows[k, :, pl.ds(width, LANES)].astype(jnp.float32), 0.0),
+            axis=1,
+            keepdims=True,
+        )
+
+        @pl.loop(0, width // 512)
+        def _(tile):
+            columns = pl.ds(pl.multiple_of(tile * 512, 512), 512)
+            value = jnp.dot(inner, down[:, columns], preferred_element_type=jnp.float32)
+            part[k, :, columns] = (value * weight).astype(jnp.bfloat16)
+
+        part_copies[k] = send(
+            part.at[k, pl.ds(4 * TOK_DEV, 4 * TOK_DEV)], part_sib.at[k], to_sib
+        )
+
+    front, back = pl.ds(0, half), pl.ds(half, half)
+    diag_copies, plane_copies = {}, {}
+
+    def add(k, r, columns, other_ref):
+        place = (k, block(r, 0), columns)
+        part[place] = (
+            part[place].astype(jnp.float32) + other_ref.astype(jnp.float32)
+        ).astype(jnp.bfloat16)
+
+    def give_diag(k):
+        part_copies[k].wait_recv()
+
+        @pl.loop(0, 4)
+        def _(r):
+            place = pl.ds(pl.multiple_of(r * TOK_DEV, TOK_DEV), TOK_DEV)
+            part[k, place, :] = (
+                part[k, place, :].astype(jnp.float32)
+                + part_sib[k, place, :].astype(jnp.float32)
+            ).astype(jnp.bfloat16)
+
+        diag_copies[k] = (
+            send(part.at[k, block(3, 0), front], diag_y.at[k], to_y),
+            send(part.at[k, block(3, 0), back], diag_x.at[k], to_x),
+        )
+        plane_copies[k] = [
+            send(part.at[k, block(1, 0), back], part_x.at[k, :, back], to_x),
+            send(part.at[k, block(2, 0), front], part_y.at[k, :, front], to_y),
+        ]
+
+    def give_plane(k):
+        from_y, from_x = diag_copies[k]
+        from_y.wait_recv()
+        add(k, 1, front, diag_y[k])
+        plane_copies[k].append(
+            send(part.at[k, block(1, 0), front], part_x.at[k, :, front], to_x)
+        )
+        from_x.wait_recv()
+        add(k, 2, back, diag_x[k])
+        plane_copies[k].append(
+            send(part.at[k, block(2, 0), back], part_y.at[k, :, back], to_y)
+        )
+
+    z_copies = {}
+
+    def give_line(k):
+        for copy in plane_copies[k]:
+            copy.wait_recv()
+        total = (
+            part[k, own, :].astype(jnp.float32)
+            + part_x[k].astype(jnp.float32)
+            + part_y[k].astype(jnp.float32)
+        )
+        if k:
+            z_out[k] = total.astype(jnp.bfloat16)
+            z_copies[k] = send(z_out.at[k], z_in.at[(4 - k) % 4], to_z[k])
+        else:
+            hidden[...] = hidden[...] + total
+
+    a, b, f, g = order
+    spread(a)
+    spread(b)
+    pass_on(a)
+    for load in loads[1:]:
+        load.wait()
+    complete(a)
+    spread(f)
+    pass_on(b)
+    experts(a)
+    complete(b)
+    spread(g)
+    pass_on(f)
+    give_diag(a)
+    experts(b)
+    complete(f)
+    pass_on(g)
+    give_plane(a)
+    give_diag(b)
+    experts(f)
+    complete(g)
+    give_line(a)
+    give_plane(b)
+    give_diag(f)
+    experts(g)
+    give_line(b)
+    give_plane(f)
+    give_diag(g)
+    give_line(f)
+    give_plane(g)
+    give_line(g)
+    total = hidden[...]
+    for k in order[1:]:
+        z_copies[k].wait_recv()
+        total = total + z_in[(4 - k) % 4].astype(jnp.float32)
+    out[...] = total.astype(jnp.bfloat16)
+    for copy in sent:
+        copy.wait_send()
+
+
 def dense_shards(
     queries,
     keys_values,
@@ -184,43 +508,69 @@
     w_up,
     w_down,
 ):
-    tensor_count = lax.axis_size("tensor")
-    expert_count = lax.axis_size("expert")
-    slot_count = tensor_count // HSPLIT
-    experts = expert_count * slot_count
-    own_expert = lax.axis_index("expert") * slot_count + lax.axis_index("tensor") // HSPLIT
+    experts = lax.axis_size("expert") * lax.axis_size("tensor") // HSPLIT
     weight_table = weight_columns(expert_ids, route_weights, experts).astype(jnp.bfloat16)
-    weight_all = lax.all_gather(weight_table, "expert", axis=0, tiled=True)
-    own_weight = lax.dynamic_slice_in_dim(weight_all, own_expert, 1, 1).astype(jnp.float32)
+    route = lax.dynamic_slice_in_dim(
+        weight_table, lax.axis_index("tensor") * TOK_DEV, TOK_DEV, 0
+    )
+    route = jnp.pad(route, ((0, 0), (0, LANES - experts)))
     attended = attend(queries, keys_values, prefix_len)
-    attended_all = lax.all_gather(attended, "expert", axis=0, tiled=True)
-    head_part = jnp.dot(attended_all, out_proj, preferred_element_type=jnp.float32)
-    head_part = head_part.astype(jnp.bfloat16).reshape(
-        expert_count, tensor_count, TOK_DEV, out_proj.shape[1]
-    )
-    head_sum = lax.psum_scatter(head_part, "tensor", scatter_dimension=1, tiled=True)
-    head_sum = lax.all_to_all(
-        head_sum.reshape(expert_count, TOK_DEV, -1), "expert", split_axis=0, concat_axis=2, tiled=True
-    )[0]
-    hidden_state = (residual.astype(jnp.float32) + head_sum.astype(jnp.float32)).astype(
-        jnp.bfloat16
-    )
-    normed = norm_rows(hidden_state, norm_gain)
-    normed_all = lax.all_gather(normed, ("expert", "tensor"), axis=0, tiled=True)
-    gate_val = jnp.dot(normed_all, w_gate[0], preferred_element_type=jnp.float32)
-    up_val = jnp.dot(normed_all, w_up[0], preferred_element_type=jnp.float32)
-    inner = (jax.nn.silu(gate_val) * up_val).astype(jnp.bfloat16)
-    result = jnp.dot(inner, w_down[0], preferred_element_type=jnp.float32)
-    part = (result * own_weight).astype(jnp.bfloat16)
-    expert_share = lax.psum_scatter(part, ("expert", "tensor"), scatter_dimension=0, tiled=True)
-    return (hidden_state.astype(jnp.float32) + expert_share.astype(jnp.float32)).astype(
-        jnp.bfloat16
+    width = residual.shape[1]
+    depth, cols = out_proj.shape
+    seq = attended.shape[0]
+    hid = w_gate.shape[2]
+    bf = jnp.bfloat16
+    vmem = pl.BlockSpec(memory_space=pltpu.VMEM)
+    hbm = pl.BlockSpec(memory_space=pl.ANY)
+    return pl.pallas_call(
+        layer_kernel,
+        out_shape=jax.ShapeDtypeStruct((TOK_DEV, width), bf),
+        in_specs=[vmem, hbm, vmem, vmem, vmem, hbm, hbm, hbm],
+        out_specs=vmem,
+        scratch_shapes=[
+            pltpu.VMEM((depth, cols), bf),
+            pltpu.VMEM((width, hid), bf),
+            pltpu.VMEM((width, hid), bf),
+            pltpu.VMEM((hid, width), bf),
+            pltpu.VMEM((3, seq, depth), bf),
+            pltpu.VMEM((4, 4, 2, TOK_DEV, cols), bf),
+            pltpu.VMEM((4, 4, TOK_DEV, cols), bf),
+            pltpu.VMEM((4, 4, TOK_DEV, cols), bf),
+            pltpu.VMEM((4, 4, TOK_DEV, cols), bf),
+            pltpu.VMEM((4, TOK_DEV, cols), bf),
+            pltpu.VMEM((4, TOK_DEV, cols), bf),
+            pltpu.VMEM((TOK_DEV, width), jnp.float32),
+            pltpu.VMEM((4, seq, width + LANES), bf),
+            pltpu.VMEM((4, seq, width), bf),
+            pltpu.VMEM((4, seq // 2, width), bf),
+            pltpu.VMEM((4, TOK_DEV, width // 2), bf),
+            pltpu.VMEM((4, TOK_DEV, width // 2), bf),
+            pltpu.VMEM((4, TOK_DEV, width), bf),
+            pltpu.VMEM((4, TOK_DEV, width), bf),
+            pltpu.VMEM((4, TOK_DEV, width), bf),
+            pltpu.VMEM((4, TOK_DEV, width), bf),
+            pltpu.SemaphoreType.DMA((COPIES,)),
+            pltpu.SemaphoreType.DMA((COPIES,)),
+            pltpu.SemaphoreType.DMA((4,)),
+        ],
+        compiler_params=pltpu.CompilerParams(
+            collective_id=0, has_side_effects=True, vmem_limit_bytes=48 * 1024 * 1024
+        ),
+    )(
+        attended,
+        out_proj,
+        residual,
+        norm_gain[None, :],
+        route,
+        w_gate[0],
+        w_up[0],
+        w_down[0],
     )
 
 
 def solution(mesh):
     experts = mesh.shape["expert"] * mesh.shape["tensor"] // HSPLIT
-    dense = experts == TOPK
+    dense = experts == TOPK and mesh.shape["expert"] == 4 and mesh.shape["tensor"] == 8
     return jax.shard_map(
         dense_shards if dense else shards,
         mesh=mesh,

time: 350 us -> 103 us (0.29)
  waiting for transfers between devices: 281 us -> 0 us
  Pallas kernels: 0 us -> 85.7 us
  matrix products: 28.3 us -> 7.21 us
  blocking collectives: 15.9 us -> 0 us
  between operations: 14.1 us -> 0.78 us
    reduce_scatter x1 -> x0, waiting for transfers between devices: 141 us -> none  [dense_shards(): lax.psum_scatter(part, ('expert', 'tensor'), scatter_dimension=0, tiled=T...]
    pallas_call x0 -> x1, Pallas kernels: none -> 85.7 us  [dense_shards(): pl.pallas_call(layer_kernel, out_shape=jax.ShapeDtypeStruct((TOK_DEV, wid...]
    all_gather x2 -> x0, waiting for transfers between devices: 81.5 us -> none  [the longest x1 52.2 us: dense_shards(): lax.all_gather(normed, ('expert', 'tensor'), axis=0, tiled=True)]
    unnamed x5 -> x0, waiting for transfers between devices: 58.4 us -> none
    dot_general x3 -> x0, matrix products: 20.4 us -> none  [the longest x1 9.73 us: dense_shards(): result = jnp.dot(inner, w_down[0], preferred_element_type=jnp.float32)]
    all_to_all x1 -> x0, blocking collectives: 8.45 us -> none  [dense_shards(): lax.all_to_all(head_sum.reshape(expert_count, TOK_DEV, -1), 'expert', spl...]
    all_gather x1 -> x0, blocking collectives: 7.47 us -> none  [dense_shards(): weight_all = lax.all_gather(weight_table, 'expert', axis=0, tiled=True)]
    unnamed x18, local copies, waits for them, and re-layouts: 1.59 us -> 6.3 us
  transfers between devices with their start and end apart: 4 -> 0, of which waited for: 4 -> 0; matrix products, arithmetic and copies ran while one was open for 0% -> 0% of each run, Pallas kernels for 0% -> 0%
where the time goes in v2:
time: 103 us
  Pallas kernels  85.7 us (83%)
  matrix products  7.21 us (7%)
  local copies, waits for them, and re-layouts  6.57 us (6%)
  other arithmetic  2.78 us (3%)
    pallas_call x1, Pallas kernels, dense_shards(): pl.pallas_call(layer_kernel, out_shape=jax.ShapeDtypeStruct((TOK_DEV, wid...  85.7 us
    unnamed x18, local copies, waits for them, and re-layouts  6.3 us
    dot_general x1, matrix products, attend(): jnp.einsum('hnc,cd->nhd', weights.astype(jnp.bfloat16), value_rows, prefe...  5.49 us

profile of v2, /device:TPU:0, one launch (start us, length us, event | category | flops | bytes accessed | tf_op | source)
XLA Modules:
  0.0 103.1 jit_solution(2878569346238476723)
XLA Ops:
  0.0 0.0 copy-start
  0.0 1.7 %copy-done = bf16[1,4,1152,256]{3,2,1,0:T(8,128)(2,1)S(1)} copy-done((bf16[1,4,1152,256]{3,2,1,0:T(8,128)(2,1)S(1)}, bf16[1,4,1152,256]{3,2,1,0:T(8,128)(2,1)}, u32[]{:S(2)}) %copy-start) | copy-done | bytes 2359320
  1.7 1.7 %convolution_multiply_fusion = f32[1152,128,8]{1,0,2:T(8,128)S(1)} fusion(bf16[1152,256]{1,0:T(8,128)(2,1)S(1)} %dynamic-slice_bitcast_fusion, bf16[128,1024]{1,0:T(8,128)(2,1)} %param.11), kind=kOutput, calls=%fused_computation.5 | convolution fusion | flops 303169536 | bytes 5275648 | tf_op jit(solution)/shard_map/nhd,cd->hnc/dot_general | solution.py:155
  3.4 0.0 copy-start.5
  4.1 1.0 %fusion.14 = pred[128,1152]{0,1:T(8,128)(4,1)S(1)} fusion(s32[1152]{0:T(1024)S(1)} %iota_add_fusion, pred[1152]{0:T(1024)(128)(4,1)S(1)} %get-tuple-element.5, pred[1152]{0:T(1024)(128)(4,1)S(1)} %get-tuple-element.6), kind=kLoop, calls=%fused_computation.18 | loop fusion | flops 442368 | bytes 154368 | tf_op jit(solution)/shard_map/or | solution.py:160
  5.2 0.4 copy-done.5
  5.6 1.7 %exponential_reduce_fusion = f32[8,128]{1,0:T(8,128)S(1)} fusion(f32[1152,128,8]{1,0,2:T(8,128)S(1)} %convolution_multiply_fusion, pred[128,1152]{0,1:T(8,128)(4,1)S(1)} %fusion.14), kind=kOutput, calls=%fused_computation.7 | output fusion | flops 4719743 | bytes 4870144 | tf_op jit(solution)/shard_map/sub | solution.py:164
  7.3 0.0 copy-start.7
  7.3 0.0 copy-start.6
  7.3 0.0 copy-start.3
  7.3 0.0 copy-start.4
  7.3 5.5 %fusion.12 = bf16[128,8,128]{0,2,1:T(8,128)(2,1)S(1)} fusion(bf16[1152,256]{1,0:T(8,128)(2,1)S(1)} %dynamic-slice_bitcast_fusion, f32[128,8]{0,1:T(8,128)S(1)} %bitcast.46, f32[1152,128,8]{1,0,2:T(8,128)} %copy-done.5, pred[128,1152]{0,1:T(8,128)(4,1)S(1)} %fusion.14), kind=kOutput, calls=%fused_computation.14 | convolution fusion | flops 306972800 | bytes 10293248 | tf_op jit(solution)/shard_map/hnc,cd->nhd/dot_general | solution.py:166
  12.8 0.1 copy.26.attended
  13.0 0.0 copy-done.7
  13.0 0.0 copy-done.6
  13.0 0.1 constant_dynamic-slice_fusion
  13.1 0.1 copy.27
  13.2 0.0 copy-done.3
  13.2 0.0 copy-done.4
  13.2 0.0 copy-start.1
  13.2 1.9 %copy-done.1 = bf16[1,4096,384]{2,1,0:T(8,128)(2,1)S(1)} copy-done((bf16[1,4096,384]{2,1,0:T(8,128)(2,1)S(1)}, bf16[1,4096,384]{2,1,0:T(8,128)(2,1)}, u32[]{:S(2)}) %copy-start.1) | copy-done | bytes 3145752
  15.1 0.0 copy-start.2
  15.1 1.6 %copy-done.2 = bf16[1024,1024]{1,0:T(8,128)(2,1)S(1)} copy-done((bf16[1024,1024]{1,0:T(8,128)(2,1)S(1)}, bf16[1024,1024]{1,0:T(8,128)(2,1)}, u32[]{:S(2)}) %copy-start.2) | copy-done | bytes 2097176
  16.7 85.7 %shard_map.109 = bf16[16,4096]{1,0:T(8,128)(2,1)S(1)} custom-call(bf16[128,1024]{1,0:T(8,128)(2,1)S(1)} %copy.26.attended, bf16[1024,1024]{1,0:T(8,128)(2,1)S(1)} %copy-done.2, bf16[16,4096]{1,0:T(8,128)(2,1)S(1)} %copy-done.3, f32[1,4096]{1,0:T(1,128)S(1)} %bitcast.42, bf16[16,128]{1,0:T(8,128)(2,1)S(1)} %pad.4.route, bf16[4096,384]{1,0:T(8,128)(2,1)S(1)} %bitcast.41, ...), custom_call_target="tpu_custom_call" | custom-call | tf_op jit(solution)/shard_map/pallas_call | solution.py:525
  102.4 0.7 copy.35
  (6 shorter events, 0.1 us)
Async XLA Ops:
  0.0 1.7 %copy-start = (bf16[1,4,1152,256]{3,2,1,0:T(8,128)(2,1)S(1)}, bf16[1,4,1152,256]{3,2,1,0:T(8,128)(2,1)}, u32[]{:S(2)}) copy-start(bf16[1,4,1152,256]{3,2,1,0:T(8,128)(2,1)} %param.12) | copy-start | bytes 7077892
  3.4 2.1 %copy-start.5 = (f32[1152,128,8]{1,0,2:T(8,128)}, f32[1152,128,8]{1,0,2:T(8,128)S(1)}, u32[]{:S(2)}) copy-start(f32[1152,128,8]{1,0,2:T(8,128)S(1)} %convolution_multiply_fusion) | copy-start | bytes 14155780
  7.3 5.7 %copy-start.7 = (bf16[128,8]{0,1:T(8,128)(2,1)S(1)}, bf16[128,8]{0,1:T(8,128)(2,1)}, u32[]{:S(2)}) copy-start(bf16[128,8]{0,1:T(8,128)(2,1)} %param.18) | copy-start | bytes 6148
  7.3 5.7 %copy-start.6 = (s32[128,8]{0,1:T(8,128)S(1)}, s32[128,8]{0,1:T(8,128)}, u32[]{:S(2)}) copy-start(s32[128,8]{0,1:T(8,128)} %param.17) | copy-start | bytes 12292
  7.3 5.9 %copy-start.3 = (bf16[16,4096]{1,0:T(8,128)(2,1)S(1)}, bf16[16,4096]{1,0:T(8,128)(2,1)}, u32[]{:S(2)}) copy-start(bf16[16,4096]{1,0:T(8,128)(2,1)} %residual.1) | copy-start | bytes 393220
  7.3 5.9 %copy-start.4 = (f32[4096]{0:T(1024)S(1)}, f32[4096]{0:T(1024)}, u32[]{:S(2)}) copy-start(f32[4096]{0:T(1024)} %param.16) | copy-start | bytes 49156
  13.2 1.9 %copy-start.1 = (bf16[1,4096,384]{2,1,0:T(8,128)(2,1)S(1)}, bf16[1,4096,384]{2,1,0:T(8,128)(2,1)}, u32[]{:S(2)}) copy-start(bf16[1,4096,384]{2,1,0:T(8,128)(2,1)} %param.19) | copy-start | bytes 9437188
  15.1 1.6 %copy-start.2 = (bf16[1024,1024]{1,0:T(8,128)(2,1)S(1)}, bf16[1024,1024]{1,0:T(8,128)(2,1)}, u32[]{:S(2)}) copy-start(bf16[1024,1024]{1,0:T(8,128)(2,1)} %proj_hbm.1) | copy-start | bytes 6291460

commit v3 on v2

--- a/solution.py
+++ b/solution.py
@@ -135,61 +135,29 @@
     return (hidden_state.astype(jnp.float32) + expert_share).astype(jnp.bfloat16)
 
 
-def weight_columns(expert_ids, route_weights, experts):
-    named_mask = expert_ids[:, :, None] == jnp.arange(experts, dtype=jnp.int32)[None, None, :]
-    return jnp.sum(
-        jnp.where(named_mask, route_weights[:, :, None].astype(jnp.float32), 0.0), axis=1
-    )
-
-
-def attend(queries, keys_values, prefix_len):
-    tensor_index = lax.axis_index("tensor")
-    step_rows = queries.shape[0]
-    per_device = queries.shape[1] // HD
-    kv_index = tensor_index * per_device // (HEADS // KVH)
-    cached = lax.dynamic_index_in_dim(keys_values[0], kv_index, 0, keepdims=False)
-    key_rows = cached[:, :HD]
-    value_rows = cached[:, HD:]
-    context = cached.shape[0]
-    query_rows = queries.reshape(step_rows, per_device, HD)
-    scores = jnp.einsum(
-        "nhd,cd->hnc", query_rows, key_rows, preferred_element_type=jnp.float32
-    ) / math.sqrt(HD)
-    columns = jnp.arange(context, dtype=jnp.int32)[None, :]
-    positions = jnp.arange(step_rows, dtype=jnp.int32)[:, None]
-    visible = ((columns < prefix_len[0]) | (columns >= PREFIX) & (columns - PREFIX <= positions))[
-        None
-    ]
-    highest = jnp.max(jnp.where(visible, scores, -1e30), axis=-1, keepdims=True)
-    weights = jnp.exp(jnp.where(visible, scores - highest, -1e30))
-    summed = jnp.sum(weights, axis=-1)
-    blended = jnp.einsum(
-        "hnc,cd->nhd", weights.astype(jnp.bfloat16), value_rows, preferred_element_type=jnp.float32
-    )
-    return (
-        (blended / jnp.transpose(summed)[:, :, None])
-        .astype(jnp.bfloat16)
-        .reshape(step_rows, per_device * HD)
-    )
-
-
 LANES = 128
 COPIES = 128
 
 
 def layer_kernel(
-    attended,
+    queries_hbm,
+    cache_hbm,
+    prefix_len,
     proj_hbm,
     residual,
     gain,
-    route,
+    expert_ids,
+    route_weights,
     gate_hbm,
     up_hbm,
     down_hbm,
     out,
+    query,
+    cached,
+    bias,
+    attended,
     proj,
-    gate,
-    up,
+    gate_up,
     down,
     seen,
     heads,
@@ -228,9 +196,19 @@
     to_sib = (e, z * 2 + (1 - c))
     to_z = [None] + [(e, line[k] * 2 + c) for k in range(1, 4)]
 
+    per_device = query.shape[1] // HD
+    hid = gate_hbm.shape[1]
+    kv_index = t * per_device // (HEADS // KVH)
     loads = []
     for index, (source, target) in enumerate(
-        ((proj_hbm, proj), (gate_hbm, gate), (up_hbm, up), (down_hbm, down))
+        (
+            (cache_hbm.at[kv_index], cached),
+            (queries_hbm, query),
+            (proj_hbm, proj),
+            (gate_hbm, gate_up.at[:, pl.ds(0, hid)]),
+            (up_hbm, gate_up.at[:, pl.ds(hid, hid)]),
+            (down_hbm, down),
+        )
     ):
         loads.append(pltpu.make_async_copy(source, target, load_sem.at[index]))
         loads[-1].start()
@@ -240,8 +218,6 @@
         pl.semaphore_signal(
             barrier, inc=1, device_id=partner, device_id_type=pl.DeviceIdType.MESH
         )
-    pl.semaphore_wait(barrier, 7)
-
     sent = []
 
     def send(source, target, partner):
@@ -258,12 +234,47 @@
         sent.append(copy)
         return copy
 
-    row_half = attended.shape[0] // 2
-    top, low = pl.ds(0, row_half), pl.ds(row_half, row_half)
-    x_top = send(attended.at[top], seen.at[0, top], to_x)
-    y_low = send(attended.at[low], seen.at[1, low], to_y)
-    x_low = send(attended.at[low], seen.at[0, low], to_x)
-    y_top = send(attended.at[top], seen.at[1, top], to_y)
+    step_rows, context = bias.shape
+    columns = lax.broadcasted_iota(jnp.int32, (step_rows, context), 1)
+    positions = lax.broadcasted_iota(jnp.int32, (step_rows, context), 0)
+    visible = (columns < prefix_len[0]) | (columns >= PREFIX) & (columns - PREFIX <= positions)
+    bias[...] = jnp.where(visible, 0.0, -1e30)
+
+    def attend_pair(pair):
+        one, two = pl.ds(2 * pair * HD, HD), pl.ds((2 * pair + 1) * HD, HD)
+        stacked = jnp.concatenate([query[:, one], query[:, two]], axis=0)
+        scores = lax.dot_general(
+            stacked,
+            cached[:, pl.ds(0, HD)],
+            (((1,), (1,)), ((), ())),
+            preferred_element_type=jnp.float32,
+        ).reshape(2, step_rows, context)
+        scores = scores + bias[...][None]
+        highest = jnp.max(scores, axis=-1, keepdims=True)
+        weights = jnp.exp((scores - highest) * (1.0 / math.sqrt(HD)))
+        summed = jnp.sum(weights, axis=-1, keepdims=True)
+        blended = jnp.dot(
+            weights.astype(jnp.bfloat16).reshape(2 * step_rows, context),
+            cached[:, pl.ds(HD, HD)],
+            preferred_element_type=jnp.float32,
+        ).reshape(2, step_rows, HD)
+        blended = (blended / summed).astype(jnp.bfloat16)
+        attended[:, one] = blended[0]
+        attended[:, two] = blended[1]
+
+    depth_half = attended.shape[1] // 2
+    top, low = pl.ds(0, depth_half), pl.ds(depth_half, depth_half)
+    loads[0].wait()
+    loads[1].wait()
+    for pair in range(per_device // 4):
+        attend_pair(pair)
+    pl.semaphore_wait(barrier, 7)
+    x_top = send(attended.at[:, top], seen.at[0, :, top], to_x)
+    y_top = send(attended.at[:, top], seen.at[1, :, top], to_y)
+    for pair in range(per_device // 4, per_device // 2):
+        attend_pair(pair)
+    y_low = send(attended.at[:, low], seen.at[1, :, low], to_y)
+    x_low = send(attended.at[:, low], seen.at[0, :, low], to_x)
 
     def project(source, r):
         @pl.loop(0, proj.shape[1] // 256)
@@ -289,17 +300,17 @@
             for k in (2, 1, 3)
         ]
 
-    loads[0].wait()
+    x_top.wait_recv()
+    d_top = send(seen.at[0, :, top], seen.at[2, :, top], to_y)
+    loads[2].wait()
     sib = [project(attended, 0), None, None, None]
-    x_top.wait_recv()
-    d_top = send(seen.at[0, top], seen.at[2, top], to_y)
+    along = [None] * 4
+    y_top.wait_recv()
     y_low.wait_recv()
-    d_low = send(seen.at[1, low], seen.at[2, low], to_x)
-    along = [None] * 4
+    d_low = send(seen.at[1, :, low], seen.at[2, :, low], to_x)
     x_low.wait_recv()
     sib[1] = project(seen.at[0], 1)
     along[0] = add_cores(0, sib[0])
-    y_top.wait_recv()
     sib[2] = project(seen.at[1], 2)
     along[1] = add_cores(1, sib[1])
     d_top.wait_recv()
@@ -333,7 +344,15 @@
     factor = lax.rsqrt(square / width + 1e-06)
     own = pl.ds(0, TOK_DEV)
     rows[0, own, pl.ds(0, width)] = (hidden[...] * factor * gain[...]).astype(jnp.bfloat16)
-    rows[0, own, pl.ds(width, LANES)] = route[...]
+    lane = lax.broadcasted_iota(jnp.int32, (TOK_DEV, LANES), 1)
+    mine = pl.ds(pl.multiple_of(t * TOK_DEV, TOK_DEV), TOK_DEV)
+    ids, gains = expert_ids[mine, :], route_weights[mine, :].astype(jnp.float32)
+    route = jnp.zeros((TOK_DEV, LANES), jnp.float32)
+    for place in range(TOPK):
+        route = route + jnp.where(
+            ids[:, place : place + 1] == lane, gains[:, place : place + 1], 0.0
+        )
+    rows[0, own, pl.ds(width, LANES)] = route.astype(jnp.bfloat16)
 
     full = rows.shape[2]
     first, last = pl.ds(0, half), pl.ds(half, full - half)
@@ -377,8 +396,8 @@
         for copy in other[k]:
             copy.wait_recv()
         values = rows.at[k, :, pl.ds(0, width)]
-        gate_val = jnp.dot(values[...], gate[...], preferred_element_type=jnp.float32)
-        up_val = jnp.dot(values[...], up[...], preferred_element_type=jnp.float32)
+        both = jnp.dot(values[...], gate_up[...], preferred_element_type=jnp.float32)
+        gate_val, up_val = both[:, :hid], both[:, hid:]
         inner = (gate_val / (1.0 + jnp.exp(-gate_val)) * up_val).astype(jnp.bfloat16)
         named = lax.broadcasted_iota(jnp.int32, (8 * TOK_DEV, LANES), 1) == own_expert
         weight = jnp.sum(
@@ -459,7 +478,7 @@
     spread(a)
     spread(b)
     pass_on(a)
-    for load in loads[1:]:
+    for load in loads[3:]:
         load.wait()
     complete(a)
     spread(f)
@@ -508,29 +527,27 @@
     w_up,
     w_down,
 ):
-    experts = lax.axis_size("expert") * lax.axis_size("tensor") // HSPLIT
-    weight_table = weight_columns(expert_ids, route_weights, experts).astype(jnp.bfloat16)
-    route = lax.dynamic_slice_in_dim(
-        weight_table, lax.axis_index("tensor") * TOK_DEV, TOK_DEV, 0
-    )
-    route = jnp.pad(route, ((0, 0), (0, LANES - experts)))
-    attended = attend(queries, keys_values, prefix_len)
     width = residual.shape[1]
     depth, cols = out_proj.shape
-    seq = attended.shape[0]
+    seq = queries.shape[0]
+    context = keys_values.shape[2]
     hid = w_gate.shape[2]
     bf = jnp.bfloat16
     vmem = pl.BlockSpec(memory_space=pltpu.VMEM)
-    hbm = pl.BlockSpec(memory_space=pl.ANY)
+    smem = pl.BlockSpec(memory_space=pltpu.SMEM)
+    hbm = pl.BlockSpec(memory_space=pltpu.HBM)
     return pl.pallas_call(
         layer_kernel,
         out_shape=jax.ShapeDtypeStruct((TOK_DEV, width), bf),
-        in_specs=[vmem, hbm, vmem, vmem, vmem, hbm, hbm, hbm],
+        in_specs=[hbm, hbm, smem, hbm, vmem, vmem, vmem, vmem, hbm, hbm, hbm],
         out_specs=vmem,
         scratch_shapes=[
+            pltpu.VMEM((seq, depth), bf),
+            pltpu.VMEM((context, 2 * HD), bf),
+            pltpu.VMEM((seq, context), jnp.float32),
+            pltpu.VMEM((seq, depth), bf),
             pltpu.VMEM((depth, cols), bf),
-            pltpu.VMEM((width, hid), bf),
-            pltpu.VMEM((width, hid), bf),
+            pltpu.VMEM((width, 2 * hid), bf),
             pltpu.VMEM((hid, width), bf),
             pltpu.VMEM((3, seq, depth), bf),
             pltpu.VMEM((4, 4, 2, TOK_DEV, cols), bf),
@@ -551,17 +568,20 @@
             pltpu.VMEM((4, TOK_DEV, width), bf),
             pltpu.SemaphoreType.DMA((COPIES,)),
             pltpu.SemaphoreType.DMA((COPIES,)),
-            pltpu.SemaphoreType.DMA((4,)),
+            pltpu.SemaphoreType.DMA((6,)),
         ],
         compiler_params=pltpu.CompilerParams(
             collective_id=0, has_side_effects=True, vmem_limit_bytes=48 * 1024 * 1024
         ),
     )(
-        attended,
+        queries,
+        keys_values[0],
+        prefix_len,
         out_proj,
         residual,
         norm_gain[None, :],
-        route,
+        expert_ids,
+        route_weights,
         w_gate[0],
         w_up[0],
         w_down[0],

time: 103 us -> 94.5 us (0.917)
  matrix products: 7.21 us -> 0 us
  other arithmetic: 2.78 us -> 0 us
  local copies, waits for them, and re-layouts: 6.57 us -> 8.07 us
    dot_general x2 -> x0, matrix products: 7.21 us -> none  [the longest x1 5.49 us: attend(): jnp.einsum('hnc,cd->nhd', weights.astype(jnp.bfloat16), value_rows, prefe...]
    unnamed x18 -> x13, local copies, waits for them, and re-layouts: 6.3 us -> 8.07 us
    sub x2 -> x0, other arithmetic: 1.71 us -> none  [the longest x1 1.71 us: attend(): weights = jnp.exp(jnp.where(visible, scores - highest, -1e+30))]
    or x1 -> x0, other arithmetic: 1.05 us -> none  [attend(): (columns < prefix_len[0]) | (columns >= PREFIX) & (columns - PREFIX <= po...]
where the time goes in v3:
time: 94.5 us; the launch traced here: 94.2 us
  Pallas kernels  85.4 us (90%)
  local copies, waits for them, and re-layouts  8.07 us (9%)
    pallas_call x1, Pallas kernels, dense_shards(): pl.pallas_call(layer_kernel, out_shape=jax.ShapeDtypeStruct((TOK_DEV, wid...  85.4 us
    unnamed x13, local copies, waits for them, and re-layouts  8.07 us

profile of v3, /device:TPU:0, one launch (start us, length us, event | category | flops | bytes accessed | tf_op | source)
XLA Modules:
  0.0 94.2 jit_solution(10232407393372850155)
XLA Ops:
  0.7 0.8 copy.13.route_weights
  1.5 0.8 copy.12.expert_ids
  2.2 0.0 copy-start
  2.2 1.7 %copy-done = bf16[1,4,1152,256]{3,2,1,0:T(8,128)(2,1)S(1)} copy-done((bf16[1,4,1152,256]{3,2,1,0:T(8,128)(2,1)S(1)}, bf16[1,4,1152,256]{3,2,1,0:T(8,128)(2,1)}, u32[]{:S(2)}) %copy-start) | copy-done | bytes 2359320
  3.9 0.0 copy-start.1
  3.9 1.6 %copy-done.1 = bf16[1024,1024]{1,0:T(8,128)(2,1)S(1)} copy-done((bf16[1024,1024]{1,0:T(8,128)(2,1)S(1)}, bf16[1024,1024]{1,0:T(8,128)(2,1)}, u32[]{:S(2)}) %copy-start.1) | copy-done | bytes 2097176
  5.5 0.0 copy-start.2
  5.5 0.9 %copy-done.2 = bf16[128,1024]{1,0:T(8,128)(2,1)S(1)} copy-done((bf16[128,1024]{1,0:T(8,128)(2,1)S(1)}, bf16[128,1024]{1,0:T(8,128)(2,1)}, u32[]{:S(2)}) %copy-start.2) | copy-done | bytes 262168
  6.4 0.0 copy-start.3
  6.5 0.9 copy-done.3
  7.4 0.0 copy-start.4
  7.4 0.7 copy-done.4
  8.1 85.4 %shard_map.109 = bf16[16,4096]{1,0:T(8,128)(2,1)S(1)} custom-call(bf16[128,1024]{1,0:T(8,128)(2,1)S(1)} %copy-done.2, bf16[4,1152,256]{2,1,0:T(8,128)(2,1)S(1)} %bitcast.5, s32[1]{0:T(128)S(6)} %copy.15.prefix_len, bf16[1024,1024]{1,0:T(8,128)(2,1)S(1)} %copy-done.1, bf16[16,4096]{1,0:T(8,128)(2,1)S(1)} %copy-done.3, f32[1,4096]{1,0:T(1,128)S(1)} %bitcast.6, ...), custom_call_target="tpu_custom_call" | custom-call | tf_op jit(solution)/shard_map/pallas_call | solution.py:539
  93.5 0.7 copy.16
Async XLA Ops:
  2.2 1.7 %copy-start = (bf16[1,4,1152,256]{3,2,1,0:T(8,128)(2,1)S(1)}, bf16[1,4,1152,256]{3,2,1,0:T(8,128)(2,1)}, u32[]{:S(2)}) copy-start(bf16[1,4,1152,256]{3,2,1,0:T(8,128)(2,1)} %param.12) | copy-start | bytes 7077892
  3.9 1.6 %copy-start.1 = (bf16[1024,1024]{1,0:T(8,128)(2,1)S(1)}, bf16[1024,1024]{1,0:T(8,128)(2,1)}, u32[]{:S(2)}) copy-start(bf16[1024,1024]{1,0:T(8,128)(2,1)} %proj_hbm.1) | copy-start | bytes 6291460
  5.5 0.9 %copy-start.2 = (bf16[128,1024]{1,0:T(8,128)(2,1)S(1)}, bf16[128,1024]{1,0:T(8,128)(2,1)}, u32[]{:S(2)}) copy-start(bf16[128,1024]{1,0:T(8,128)(2,1)} %queries_hbm.1) | copy-start | bytes 786436
  6.4 0.9 copy-start.3
  7.4 0.7 copy-start.4

commit v4 on v3

--- a/solution.py
+++ b/solution.py
@@ -136,18 +136,17 @@
 
 
 LANES = 128
+EXTRA = 64
 COPIES = 128
 
 
 def layer_kernel(
     queries_hbm,
     cache_hbm,
-    prefix_len,
+    table,
     proj_hbm,
-    residual,
-    gain,
-    expert_ids,
-    route_weights,
+    residual_hbm,
+    gain_hbm,
     gate_hbm,
     up_hbm,
     down_hbm,
@@ -157,15 +156,17 @@
     bias,
     attended,
     proj,
+    residual,
+    gain,
     gate_up,
     down,
+    tables,
     seen,
     heads,
     heads_sib,
     head_sum,
     heads_z,
-    col_out,
-    col_in,
+    res_in,
     hidden,
     rows,
     part,
@@ -204,6 +205,8 @@
         (
             (cache_hbm.at[kv_index], cached),
             (queries_hbm, query),
+            (residual_hbm, residual),
+            (gain_hbm, gain),
             (proj_hbm, proj),
             (gate_hbm, gate_up.at[:, pl.ds(0, hid)]),
             (up_hbm, gate_up.at[:, pl.ds(hid, hid)]),
@@ -237,7 +240,8 @@
     step_rows, context = bias.shape
     columns = lax.broadcasted_iota(jnp.int32, (step_rows, context), 1)
     positions = lax.broadcasted_iota(jnp.int32, (step_rows, context), 0)
-    visible = (columns < prefix_len[0]) | (columns >= PREFIX) & (columns - PREFIX <= positions)
+    live = table[0:1, EXTRA : EXTRA + 1].astype(jnp.int32)
+    visible = (columns < live) | (columns >= PREFIX) & (columns - PREFIX <= positions)
     bias[...] = jnp.where(visible, 0.0, -1e30)
 
     def attend_pair(pair):
@@ -271,6 +275,17 @@
     pl.semaphore_wait(barrier, 7)
     x_top = send(attended.at[:, top], seen.at[0, :, top], to_x)
     y_top = send(attended.at[:, top], seen.at[1, :, top], to_y)
+    quarter = width // 4
+
+    def column_block(r):
+        return pl.ds(pl.multiple_of(flat[r] * quarter, quarter), quarter)
+
+    loads[2].wait()
+    tables[e] = table[...].astype(jnp.bfloat16).reshape(tables.shape[1:])
+    early = []
+    for r in (1, 2, 3):
+        early.append(send(residual.at[:, column_block(r)], res_in.at[r], (flat[r], t)))
+        early.append(send(tables.at[e], tables.at[e], (flat[r], t)))
     for pair in range(per_device // 4, per_device // 2):
         attend_pair(pair)
     y_low = send(attended.at[:, low], seen.at[1, :, low], to_y)
@@ -302,7 +317,8 @@
 
     x_top.wait_recv()
     d_top = send(seen.at[0, :, top], seen.at[2, :, top], to_y)
-    loads[2].wait()
+    loads[3].wait()
+    loads[4].wait()
     sib = [project(attended, 0), None, None, None]
     along = [None] * 4
     y_top.wait_recv()
@@ -319,108 +335,103 @@
     along[2] = add_cores(2, sib[2])
     along[3] = add_cores(3, sib[3])
 
-    columns_in = [None] * 4
-    for r in (1, 2, 3, 0):
+    pairs = (y, 1 - y)
+    order = (0, 1, 3, 2)
+    z_rows, x_rows, y_rows, d_first, d_last = {}, {}, {}, {}, {}
+    other = {}
+
+    def state(r, place):
         for copy in along[r]:
             copy.wait_recv()
         total = head_sum[r, z].astype(jnp.float32)
         for k in range(1, 4):
             total = total + heads_z[r, k].astype(jnp.float32)
-        if r:
-            col_out[r] = total.astype(jnp.bfloat16)
-            columns_in[r] = send(col_out.at[r], col_in.at[r], (flat[r], t))
-        else:
-            col_in[0] = total.astype(jnp.bfloat16)
-    quarter = width // 4
-    square = jnp.zeros((TOK_DEV, 1), jnp.float32)
-    for r in range(4):
-        if r:
-            columns_in[r].wait_recv()
-        columns = pl.ds(pl.multiple_of(flat[r] * quarter, quarter), quarter)
-        state = residual[:, columns].astype(jnp.float32) + col_in[r].astype(jnp.float32)
-        state = state.astype(jnp.bfloat16).astype(jnp.float32)
-        hidden[:, columns] = state
-        square = square + jnp.sum(state * state, axis=1, keepdims=True)
-    factor = lax.rsqrt(square / width + 1e-06)
-    own = pl.ds(0, TOK_DEV)
-    rows[0, own, pl.ds(0, width)] = (hidden[...] * factor * gain[...]).astype(jnp.bfloat16)
-    lane = lax.broadcasted_iota(jnp.int32, (TOK_DEV, LANES), 1)
-    mine = pl.ds(pl.multiple_of(t * TOK_DEV, TOK_DEV), TOK_DEV)
-    ids, gains = expert_ids[mine, :], route_weights[mine, :].astype(jnp.float32)
-    route = jnp.zeros((TOK_DEV, LANES), jnp.float32)
-    for place in range(TOPK):
-        route = route + jnp.where(
-            ids[:, place : place + 1] == lane, gains[:, place : place + 1], 0.0
-        )
-    rows[0, own, pl.ds(width, LANES)] = route.astype(jnp.bfloat16)
-
-    full = rows.shape[2]
-    first, last = pl.ds(0, half), pl.ds(half, full - half)
-
-    def block(r, d):
-        return pl.ds((d * 4 + r) * TOK_DEV, TOK_DEV)
-
-    order = (0, 1, 3, 2)
-    z_rows = [None] + [
-        send(rows.at[0, own], rows.at[(4 - k) % 4, own], to_z[k]) for k in range(1, 4)
-    ]
-    x_rows, y_rows, d_first, d_last = {}, {}, {}, {}
-    other = {k: [] for k in order}
+        own = residual[:, column_block(0)] if r == 0 else res_in[r]
+        rows[(0, 0, 0, *place)] = (total + own.astype(jnp.float32)).astype(jnp.bfloat16)
+
+    def launch(h):
+        piece = rows.at[0, 0, 0, pairs[h]]
+        for k in (2, 1, 3):
+            z_rows[k, h] = send(piece, rows.at[(4 - k) % 4, 0, 0, pairs[h]], to_z[k])
+        x_rows[0, h] = send(piece, rows.at[0, 1, 0, pairs[h]], to_x)
+        y_rows[0, h] = send(piece, rows.at[0, 2, 0, pairs[h]], to_y)
+
+    def share(k, r):
+        other[k, r] = send(rows.at[k, r, 0], rows.at[k, r, 1], to_sib)
 
     def spread(k):
-        if k:
-            z_rows[(4 - k) % 4].wait_recv()
-        x_rows[k] = send(rows.at[k, own], rows.at[k, block(1, 0)], to_x)
-        y_rows[k] = send(rows.at[k, own], rows.at[k, block(2, 0)], to_y)
-        other[k].append(send(rows.at[k, own], rows.at[k, block(0, 1)], to_sib))
+        for h in (0, 1):
+            z_rows[(4 - k) % 4, h].wait_recv()
+            piece = rows.at[k, 0, 0, pairs[h]]
+            x_rows[k, h] = send(piece, rows.at[k, 1, 0, pairs[h]], to_x)
+            y_rows[k, h] = send(piece, rows.at[k, 2, 0, pairs[h]], to_y)
+        share(k, 0)
 
     def pass_on(k):
-        x_rows[k].wait_recv()
-        d_first[k] = send(
-            rows.at[k, block(1, 0), first], rows.at[k, block(3, 0), first], to_y
-        )
-        other[k].append(send(rows.at[k, block(1, 0)], rows.at[k, block(1, 1)], to_sib))
-        y_rows[k].wait_recv()
-        d_last[k] = send(rows.at[k, block(2, 0), last], rows.at[k, block(3, 0), last], to_x)
-        other[k].append(send(rows.at[k, block(2, 0)], rows.at[k, block(2, 1)], to_sib))
+        x_rows[k, 0].wait_recv()
+        d_first[k] = send(rows.at[k, 1, 0, y], rows.at[k, 3, 0, y], to_y)
+        y_rows[k, 0].wait_recv()
+        y_rows[k, 1].wait_recv()
+        d_last[k] = send(rows.at[k, 2, 0, y], rows.at[k, 3, 0, y], to_x)
+        x_rows[k, 1].wait_recv()
+        share(k, 1)
+        share(k, 2)
 
     def complete(k):
         d_first[k].wait_recv()
         d_last[k].wait_recv()
-        other[k].append(send(rows.at[k, block(3, 0)], rows.at[k, block(3, 1)], to_sib))
+        share(k, 3)
+
+    for copy in early:
+        copy.wait_recv()
+    state(0, (y, x))
+    state(1, (y, 1 - x))
+    launch(0)
+    state(2, (1 - y, x))
+    state(3, (1 - y, 1 - x))
+    launch(1)
+    share(0, 0)
 
     own_expert = e * 2 + t // HSPLIT
+    slab = 8 * TOK_DEV
     part_copies = {}
 
     def experts(k):
-        for copy in other[k]:
-            copy.wait_recv()
-        values = rows.at[k, :, pl.ds(0, width)]
-        both = jnp.dot(values[...], gate_up[...], preferred_element_type=jnp.float32)
+        square = jnp.zeros((slab, 1), jnp.float32)
+        both = jnp.zeros((slab, 2 * hid), jnp.float32)
+        for r in range(4):
+            other[k, r].wait_recv()
+            values = rows[k, r].reshape(slab, quarter).astype(jnp.float32)
+            square = square + jnp.sum(values * values, axis=1, keepdims=True)
+            scaled = (values * gain[:, column_block(r)]).astype(jnp.bfloat16)
+            both = both + jnp.dot(
+                scaled, gate_up[column_block(r), :], preferred_element_type=jnp.float32
+            )
+        both = both * lax.rsqrt(square / width + 1e-06)
         gate_val, up_val = both[:, :hid], both[:, hid:]
         inner = (gate_val / (1.0 + jnp.exp(-gate_val)) * up_val).astype(jnp.bfloat16)
-        named = lax.broadcasted_iota(jnp.int32, (8 * TOK_DEV, LANES), 1) == own_expert
-        weight = jnp.sum(
-            jnp.where(named, rows[k, :, pl.ds(width, LANES)].astype(jnp.float32), 0.0),
-            axis=1,
-            keepdims=True,
-        )
+        named = lax.broadcasted_iota(jnp.int32, (slab, LANES), 1) == own_expert
+        listed = jnp.concatenate(
+            [tables[s, line[k] * 2 + core] for core in (c, 1 - c) for s in range(4)], axis=0
+        )
+        weight = jnp.sum(jnp.where(named, listed.astype(jnp.float32), 0.0), axis=1, keepdims=True)
 
         @pl.loop(0, width // 512)
         def _(tile):
             columns = pl.ds(pl.multiple_of(tile * 512, 512), 512)
             value = jnp.dot(inner, down[:, columns], preferred_element_type=jnp.float32)
-            part[k, :, columns] = (value * weight).astype(jnp.bfloat16)
-
-        part_copies[k] = send(
-            part.at[k, pl.ds(4 * TOK_DEV, 4 * TOK_DEV)], part_sib.at[k], to_sib
-        )
-
+            part[k, :, :, :, columns] = (
+                (value * weight).astype(jnp.bfloat16).reshape(2, 4, TOK_DEV, 512)
+            )
+
+        part_copies[k] = send(part.at[k, 1], part_sib.at[k], to_sib)
+
+    half = width // 2
     front, back = pl.ds(0, half), pl.ds(half, half)
     diag_copies, plane_copies = {}, {}
 
     def add(k, r, columns, other_ref):
-        place = (k, block(r, 0), columns)
+        place = (k, 0, flat[r], slice(None), columns)
         part[place] = (
             part[place].astype(jnp.float32) + other_ref.astype(jnp.float32)
         ).astype(jnp.bfloat16)
@@ -429,20 +440,18 @@
         part_copies[k].wait_recv()
 
         @pl.loop(0, 4)
-        def _(r):
-            place = pl.ds(pl.multiple_of(r * TOK_DEV, TOK_DEV), TOK_DEV)
-            part[k, place, :] = (
-                part[k, place, :].astype(jnp.float32)
-                + part_sib[k, place, :].astype(jnp.float32)
+        def _(s):
+            part[k, 0, s] = (
+                part[k, 0, s].astype(jnp.float32) + part_sib[k, s].astype(jnp.float32)
             ).astype(jnp.bfloat16)
 
         diag_copies[k] = (
-            send(part.at[k, block(3, 0), front], diag_y.at[k], to_y),
-            send(part.at[k, block(3, 0), back], diag_x.at[k], to_x),
+            send(part.at[k, 0, flat[3], :, front], diag_y.at[k], to_y),
+            send(part.at[k, 0, flat[3], :, back], diag_x.at[k], to_x),
         )
         plane_copies[k] = [
-            send(part.at[k, block(1, 0), back], part_x.at[k, :, back], to_x),
-            send(part.at[k, block(2, 0), front], part_y.at[k, :, front], to_y),
+            send(part.at[k, 0, flat[1], :, back], part_x.at[k, :, back], to_x),
+            send(part.at[k, 0, flat[2], :, front], part_y.at[k, :, front], to_y),
         ]
 
     def give_plane(k):
@@ -450,12 +459,12 @@
         from_y.wait_recv()
         add(k, 1, front, diag_y[k])
         plane_copies[k].append(
-            send(part.at[k, block(1, 0), front], part_x.at[k, :, front], to_x)
+            send(part.at[k, 0, flat[1], :, front], part_x.at[k, :, front], to_x)
         )
         from_x.wait_recv()
         add(k, 2, back, diag_x[k])
         plane_copies[k].append(
-            send(part.at[k, block(2, 0), back], part_y.at[k, :, back], to_y)
+            send(part.at[k, 0, flat[2], :, back], part_y.at[k, :, back], to_y)
         )
 
     z_copies = {}
@@ -464,7 +473,7 @@
         for copy in plane_copies[k]:
             copy.wait_recv()
         total = (
-            part[k, own, :].astype(jnp.float32)
+            part[k, 0, e].astype(jnp.float32)
             + part_x[k].astype(jnp.float32)
             + part_y[k].astype(jnp.float32)
         )
@@ -472,13 +481,12 @@
             z_out[k] = total.astype(jnp.bfloat16)
             z_copies[k] = send(z_out.at[k], z_in.at[(4 - k) % 4], to_z[k])
         else:
-            hidden[...] = hidden[...] + total
+            hidden[...] = total
 
     a, b, f, g = order
-    spread(a)
     spread(b)
     pass_on(a)
-    for load in loads[3:]:
+    for load in loads[5:]:
         load.wait()
     complete(a)
     spread(f)
@@ -509,7 +517,12 @@
     for k in order[1:]:
         z_copies[k].wait_recv()
         total = total + z_in[(4 - k) % 4].astype(jnp.float32)
-    out[...] = total.astype(jnp.bfloat16)
+    hidden[...] = total
+    for r in range(4):
+        columns = column_block(r)
+        out[:, columns] = (
+            hidden[:, columns] + rows[0, r, 0, y, x].astype(jnp.float32)
+        ).astype(jnp.bfloat16)
     for copy in sent:
         copy.wait_send()
 
@@ -527,6 +540,12 @@
     w_up,
     w_down,
 ):
+    lanes = jnp.arange(LANES, dtype=jnp.int32)
+    named_mask = expert_ids[:, :, None] == lanes[None, None, :]
+    table = jnp.sum(
+        jnp.where(named_mask, route_weights[:, :, None].astype(jnp.float32), 0.0), axis=1
+    )
+    table = jnp.where(lanes[None, :] == EXTRA, prefix_len.astype(jnp.float32)[:, None], table)
     width = residual.shape[1]
     depth, cols = out_proj.shape
     seq = queries.shape[0]
@@ -534,12 +553,11 @@
     hid = w_gate.shape[2]
     bf = jnp.bfloat16
     vmem = pl.BlockSpec(memory_space=pltpu.VMEM)
-    smem = pl.BlockSpec(memory_space=pltpu.SMEM)
     hbm = pl.BlockSpec(memory_space=pltpu.HBM)
     return pl.pallas_call(
         layer_kernel,
         out_shape=jax.ShapeDtypeStruct((TOK_DEV, width), bf),
-        in_specs=[hbm, hbm, smem, hbm, vmem, vmem, vmem, vmem, hbm, hbm, hbm],
+        in_specs=[hbm, hbm, vmem, hbm, hbm, hbm, hbm, hbm, hbm],
         out_specs=vmem,
         scratch_shapes=[
             pltpu.VMEM((seq, depth), bf),
@@ -547,19 +565,21 @@
             pltpu.VMEM((seq, context), jnp.float32),
             pltpu.VMEM((seq, depth), bf),
             pltpu.VMEM((depth, cols), bf),
+            pltpu.VMEM((TOK_DEV, width), bf),
+            pltpu.VMEM((1, width), jnp.float32),
             pltpu.VMEM((width, 2 * hid), bf),
             pltpu.VMEM((hid, width), bf),
+            pltpu.VMEM((4, 8, TOK_DEV, LANES), bf),
             pltpu.VMEM((3, seq, depth), bf),
             pltpu.VMEM((4, 4, 2, TOK_DEV, cols), bf),
             pltpu.VMEM((4, 4, TOK_DEV, cols), bf),
             pltpu.VMEM((4, 4, TOK_DEV, cols), bf),
             pltpu.VMEM((4, 4, TOK_DEV, cols), bf),
             pltpu.VMEM((4, TOK_DEV, cols), bf),
-            pltpu.VMEM((4, TOK_DEV, cols), bf),
             pltpu.VMEM((TOK_DEV, width), jnp.float32),
-            pltpu.VMEM((4, seq, width + LANES), bf),
-            pltpu.VMEM((4, seq, width), bf),
-            pltpu.VMEM((4, seq // 2, width), bf),
+            pltpu.VMEM((4, 4, 2, 2, 2, TOK_DEV, cols), bf),
+            pltpu.VMEM((4, 2, 4, TOK_DEV, width), bf),
+            pltpu.VMEM((4, 4, TOK_DEV, width), bf),
             pltpu.VMEM((4, TOK_DEV, width // 2), bf),
             pltpu.VMEM((4, TOK_DEV, width // 2), bf),
             pltpu.VMEM((4, TOK_DEV, width), bf),
@@ -568,7 +588,7 @@
             pltpu.VMEM((4, TOK_DEV, width), bf),
             pltpu.SemaphoreType.DMA((COPIES,)),
             pltpu.SemaphoreType.DMA((COPIES,)),
-            pltpu.SemaphoreType.DMA((6,)),
+            pltpu.SemaphoreType.DMA((8,)),
         ],
         compiler_params=pltpu.CompilerParams(
             collective_id=0, has_side_effects=True, vmem_limit_bytes=48 * 1024 * 1024
@@ -576,12 +596,10 @@
     )(
         queries,
         keys_values[0],
-        prefix_len,
+        table,
         out_proj,
         residual,
         norm_gain[None, :],
-        expert_ids,
-        route_weights,
         w_gate[0],
         w_up[0],
         w_down[0],

time: 94.5 us -> 92.2 us (0.976)
  Pallas kernels: 85.4 us -> 82.7 us
    pallas_call x1, Pallas kernels: 85.4 us -> 82.7 us  [dense_shards(): pl.pallas_call(layer_kernel, out_shape=jax.ShapeDtypeStruct((TOK_DEV, wid...]
    unnamed x13 -> x12, local copies, waits for them, and re-layouts: 8.07 us -> 7.27 us
where the time goes in v4:
time: 92.2 us; the launch traced here: 91.8 us
  Pallas kernels  82.7 us (90%)
  local copies, waits for them, and re-layouts  8.05 us (9%)
    pallas_call x1, Pallas kernels, dense_shards(): pl.pallas_call(layer_kernel, out_shape=jax.ShapeDtypeStruct((TOK_DEV, wid...  82.7 us
    unnamed x12, local copies, waits for them, and re-layouts  7.27 us

profile of v4, /device:TPU:0, one launch (start us, length us, event | category | flops | bytes accessed | tf_op | source)
XLA Modules:
  0.0 91.8 jit_solution(2590467526372740953)
XLA Ops:
  0.7 0.8 copy.14
  1.5 0.8 copy.15
  2.2 0.3 select_reduce_fusion
  2.6 0.0 copy-start
  2.6 1.7 %copy-done = bf16[1,4,1152,256]{3,2,1,0:T(8,128)(2,1)S(1)} copy-done((bf16[1,4,1152,256]{3,2,1,0:T(8,128)(2,1)S(1)}, bf16[1,4,1152,256]{3,2,1,0:T(8,128)(2,1)}, u32[]{:S(2)}) %copy-start) | copy-done | bytes 2359320
  4.3 0.0 copy-start.1
  4.3 1.6 %copy-done.1 = bf16[1024,1024]{1,0:T(8,128)(2,1)S(1)} copy-done((bf16[1024,1024]{1,0:T(8,128)(2,1)S(1)}, bf16[1024,1024]{1,0:T(8,128)(2,1)}, u32[]{:S(2)}) %copy-start.1) | copy-done | bytes 2097176
  5.9 0.0 copy-start.2
  5.9 0.9 %copy-done.2 = bf16[128,1024]{1,0:T(8,128)(2,1)S(1)} copy-done((bf16[128,1024]{1,0:T(8,128)(2,1)S(1)}, bf16[128,1024]{1,0:T(8,128)(2,1)}, u32[]{:S(2)}) %copy-start.2) | copy-done | bytes 262168
  6.8 0.0 copy-start.3
  6.8 0.9 copy-done.3
  7.7 0.0 copy-start.4
  7.7 0.7 copy-done.4
  8.4 82.7 %shard_map.109 = bf16[16,4096]{1,0:T(8,128)(2,1)S(1)} custom-call(bf16[128,1024]{1,0:T(8,128)(2,1)S(1)} %copy-done.2, bf16[4,1152,256]{2,1,0:T(8,128)(2,1)S(1)} %bitcast.6, f32[128,128]{1,0:T(8,128)S(1)} %broadcast_select_fusion.table, bf16[1024,1024]{1,0:T(8,128)(2,1)S(1)} %copy-done.1, bf16[16,4096]{1,0:T(8,128)(2,1)S(1)} %copy-done.3, ...), custom_call_target="tpu_custom_call" | custom-call | tf_op jit(solution)/shard_map/pallas_call | solution.py:557
  91.2 0.7 copy.18
  (2 shorter events, 0.0 us)
Async XLA Ops:
  2.6 1.7 %copy-start = (bf16[1,4,1152,256]{3,2,1,0:T(8,128)(2,1)S(1)}, bf16[1,4,1152,256]{3,2,1,0:T(8,128)(2,1)}, u32[]{:S(2)}) copy-start(bf16[1,4,1152,256]{3,2,1,0:T(8,128)(2,1)} %param.12) | copy-start | bytes 7077892
  4.3 1.6 %copy-start.1 = (bf16[1024,1024]{1,0:T(8,128)(2,1)S(1)}, bf16[1024,1024]{1,0:T(8,128)(2,1)}, u32[]{:S(2)}) copy-start(bf16[1024,1024]{1,0:T(8,128)(2,1)} %proj_hbm.1) | copy-start | bytes 6291460
  5.9 0.9 %copy-start.2 = (bf16[128,1024]{1,0:T(8,128)(2,1)S(1)}, bf16[128,1024]{1,0:T(8,128)(2,1)}, u32[]{:S(2)}) copy-start(bf16[128,1024]{1,0:T(8,128)(2,1)} %queries_hbm.1) | copy-start | bytes 786436
  6.8 0.9 copy-start.3
  7.7 0.7 copy-start.4

commit v5 on v4

--- a/solution.py
+++ b/solution.py
@@ -136,14 +136,15 @@
 
 
 LANES = 128
-EXTRA = 64
 COPIES = 128
 
 
 def layer_kernel(
     queries_hbm,
     cache_hbm,
-    table,
+    prefix_len,
+    ids_hbm,
+    gains_hbm,
     proj_hbm,
     residual_hbm,
     gain_hbm,
@@ -160,6 +161,8 @@
     gain,
     gate_up,
     down,
+    ids,
+    gains,
     tables,
     seen,
     heads,
@@ -211,10 +214,13 @@
             (gate_hbm, gate_up.at[:, pl.ds(0, hid)]),
             (up_hbm, gate_up.at[:, pl.ds(hid, hid)]),
             (down_hbm, down),
+            (ids_hbm, ids),
+            (gains_hbm, gains),
         )
     ):
         loads.append(pltpu.make_async_copy(source, target, load_sem.at[index]))
-        loads[-1].start()
+    for index in (0, 1, 8, 9, 2, 3, 4, 5, 6, 7):
+        loads[index].start()
 
     barrier = pltpu.get_barrier_semaphore()
     for partner in (to_x, to_y, to_diag, to_sib, *to_z[1:]):
@@ -240,8 +246,7 @@
     step_rows, context = bias.shape
     columns = lax.broadcasted_iota(jnp.int32, (step_rows, context), 1)
     positions = lax.broadcasted_iota(jnp.int32, (step_rows, context), 0)
-    live = table[0:1, EXTRA : EXTRA + 1].astype(jnp.int32)
-    visible = (columns < live) | (columns >= PREFIX) & (columns - PREFIX <= positions)
+    visible = (columns < prefix_len[0]) | (columns >= PREFIX) & (columns - PREFIX <= positions)
     bias[...] = jnp.where(visible, 0.0, -1e30)
 
     def attend_pair(pair):
@@ -281,7 +286,23 @@
         return pl.ds(pl.multiple_of(flat[r] * quarter, quarter), quarter)
 
     loads[2].wait()
-    tables[e] = table[...].astype(jnp.bfloat16).reshape(tables.shape[1:])
+    loads[8].wait()
+    loads[9].wait()
+    along_rows = lax.broadcasted_iota(jnp.int32, (LANES, step_rows), 0)
+    along_lanes = lax.broadcasted_iota(jnp.int32, (LANES, step_rows), 1)
+    turned = jnp.zeros((LANES, step_rows), jnp.float32)
+    for place in range(TOPK):
+        turned = turned + jnp.where(
+            ids[place : place + 1, :] == along_rows, gains[place : place + 1, :], 0.0
+        )
+    unit = jnp.where(along_rows == along_lanes, 1.0, 0.0).astype(jnp.bfloat16)
+    table = lax.dot_general(
+        unit,
+        turned.astype(jnp.bfloat16),
+        (((1,), (1,)), ((), ())),
+        preferred_element_type=jnp.float32,
+    )
+    tables[e] = table.astype(jnp.bfloat16).reshape(tables.shape[1:])
     early = []
     for r in (1, 2, 3):
         early.append(send(residual.at[:, column_block(r)], res_in.at[r], (flat[r], t)))
@@ -486,33 +507,33 @@
     a, b, f, g = order
     spread(b)
     pass_on(a)
-    for load in loads[5:]:
-        load.wait()
     complete(a)
     spread(f)
     pass_on(b)
+    for load in loads[5:8]:
+        load.wait()
     experts(a)
     complete(b)
     spread(g)
     pass_on(f)
-    give_diag(a)
     experts(b)
     complete(f)
     pass_on(g)
-    give_plane(a)
     give_diag(b)
     experts(f)
     complete(g)
-    give_line(a)
     give_plane(b)
     give_diag(f)
     experts(g)
     give_line(b)
     give_plane(f)
     give_diag(g)
+    give_diag(a)
     give_line(f)
     give_plane(g)
+    give_plane(a)
     give_line(g)
+    give_line(a)
     total = hidden[...]
     for k in order[1:]:
         z_copies[k].wait_recv()
@@ -540,12 +561,6 @@
     w_up,
     w_down,
 ):
-    lanes = jnp.arange(LANES, dtype=jnp.int32)
-    named_mask = expert_ids[:, :, None] == lanes[None, None, :]
-    table = jnp.sum(
-        jnp.where(named_mask, route_weights[:, :, None].astype(jnp.float32), 0.0), axis=1
-    )
-    table = jnp.where(lanes[None, :] == EXTRA, prefix_len.astype(jnp.float32)[:, None], table)
     width = residual.shape[1]
     depth, cols = out_proj.shape
     seq = queries.shape[0]
@@ -553,11 +568,12 @@
     hid = w_gate.shape[2]
     bf = jnp.bfloat16
     vmem = pl.BlockSpec(memory_space=pltpu.VMEM)
+    smem = pl.BlockSpec(memory_space=pltpu.SMEM)
     hbm = pl.BlockSpec(memory_space=pltpu.HBM)
     return pl.pallas_call(
         layer_kernel,
         out_shape=jax.ShapeDtypeStruct((TOK_DEV, width), bf),
-        in_specs=[hbm, hbm, vmem, hbm, hbm, hbm, hbm, hbm, hbm],
+        in_specs=[hbm, hbm, smem, hbm, hbm, hbm, hbm, hbm, hbm, hbm, hbm],
         out_specs=vmem,
         scratch_shapes=[
             pltpu.VMEM((seq, depth), bf),
@@ -569,6 +585,8 @@
             pltpu.VMEM((1, width), jnp.float32),
             pltpu.VMEM((width, 2 * hid), bf),
             pltpu.VMEM((hid, width), bf),
+            pltpu.VMEM((TOPK, seq), jnp.int32),
+            pltpu.VMEM((TOPK, seq), jnp.float32),
             pltpu.VMEM((4, 8, TOK_DEV, LANES), bf),
             pltpu.VMEM((3, seq, depth), bf),
             pltpu.VMEM((4, 4, 2, TOK_DEV, cols), bf),
@@ -588,15 +606,17 @@
             pltpu.VMEM((4, TOK_DEV, width), bf),
             pltpu.SemaphoreType.DMA((COPIES,)),
             pltpu.SemaphoreType.DMA((COPIES,)),
-            pltpu.SemaphoreType.DMA((8,)),
+            pltpu.SemaphoreType.DMA((10,)),
         ],
         compiler_params=pltpu.CompilerParams(
-            collective_id=0, has_side_effects=True, vmem_limit_bytes=48 * 1024 * 1024
+            collective_id=0, has_side_effects=True, vmem_limit_bytes=63 * 1024 * 1024
         ),
     )(
         queries,
         keys_values[0],
-        table,
+        prefix_len,
+        expert_ids.T,
+        route_weights.T.astype(jnp.float32),
         out_proj,
         residual,
         norm_gain[None, :],

time: 92.2 us -> 86.7 us (0.940)
  the two profiles are of different devices: /device:TPU:0 before, /device:TPU:25 now
where the time goes in v5:
time: 86.7 us; the launch traced here: 86.5 us
  Pallas kernels  83 us (96%)
  local copies, waits for them, and re-layouts  1.57 us (2%)
  other arithmetic  1.28 us (1%)
    pallas_call x1, Pallas kernels, dense_shards(): pl.pallas_call(layer_kernel, out_shape=jax.ShapeDtypeStruct((TOK_DEV, wid...  83 us

profile of v5, /device:TPU:25, one launch (start us, length us, event | category | flops | bytes accessed | tf_op | source)
XLA Modules:
  0.0 86.5 jit_solution(15468588644082210156)
XLA Ops:
  0.7 1.3 %convert_bitcast_fusion.gains_hbm = f32[8,128]{1,0:T(8,128)} fusion(bf16[128,8]{0,1:T(8,128)(2,1)} %param.18), kind=kLoop, calls=%fused_computation | loop fusion | flops 1024 | bytes 6144 | tf_op jit(solution)/shard_map/convert_element_type | solution.py:619
  1.9 83.0 %shard_map.109 = bf16[16,4096]{1,0:T(8,128)(2,1)} custom-call(bf16[128,1024]{1,0:T(8,128)(2,1)} %queries_hbm.1, bf16[4,1152,256]{2,1,0:T(8,128)(2,1)} %bitcast.11, s32[1]{0:T(128)S(6)} %copy.13.prefix_len, s32[8,128]{1,0:T(8,128)} %bitcast.13, f32[8,128]{1,0:T(8,128)} %convert_bitcast_fusion.gains_hbm, bf16[1024,1024]{1,0:T(8,128)(2,1)} %proj_hbm.1, ...), custom_call_target="tpu_custom_call" | custom-call | tf_op jit(solution)/shard_map/pallas_call | solution.py:573
  85.0 1.6 %copy.14 = bf16[16,4096]{1,0:T(8,128)(2,1)} copy(bf16[16,4096]{1,0:T(8,128)(2,1)} %shard_map.109) | data formatting | bytes 262144

commit v6 on v5

--- a/solution.py
+++ b/solution.py
@@ -415,6 +415,8 @@
 
     own_expert = e * 2 + t // HSPLIT
     slab = 8 * TOK_DEV
+    half = width // 2
+    front, back = pl.ds(0, half), pl.ds(half, half)
     part_copies = {}
 
     def experts(k):
@@ -437,18 +439,23 @@
         )
         weight = jnp.sum(jnp.where(named, listed.astype(jnp.float32), 0.0), axis=1, keepdims=True)
 
-        @pl.loop(0, width // 512)
-        def _(tile):
-            columns = pl.ds(pl.multiple_of(tile * 512, 512), 512)
-            value = jnp.dot(inner, down[:, columns], preferred_element_type=jnp.float32)
-            part[k, :, :, :, columns] = (
-                (value * weight).astype(jnp.bfloat16).reshape(2, 4, TOK_DEV, 512)
+        part_copies[k] = []
+        for columns_half in (front, back):
+
+            @pl.loop(columns_half.start // 512, (columns_half.start + half) // 512)
+            def _(tile):
+                columns = pl.ds(pl.multiple_of(tile * 512, 512), 512)
+                value = jnp.dot(inner, down[:, columns], preferred_element_type=jnp.float32)
+                part[k, :, :, :, columns] = (
+                    (value * weight).astype(jnp.bfloat16).reshape(2, 4, TOK_DEV, 512)
+                )
+
+            part_copies[k].append(
+                send(
+                    part.at[k, 1, :, :, columns_half], part_sib.at[k, :, :, columns_half], to_sib
+                )
             )
 
-        part_copies[k] = send(part.at[k, 1], part_sib.at[k], to_sib)
-
-    half = width // 2
-    front, back = pl.ds(0, half), pl.ds(half, half)
     diag_copies, plane_copies = {}, {}
 
     def add(k, r, columns, other_ref):
@@ -458,22 +465,26 @@
         ).astype(jnp.bfloat16)
 
     def give_diag(k):
-        part_copies[k].wait_recv()
-
-        @pl.loop(0, 4)
-        def _(s):
-            part[k, 0, s] = (
-                part[k, 0, s].astype(jnp.float32) + part_sib[k, s].astype(jnp.float32)
-            ).astype(jnp.bfloat16)
-
-        diag_copies[k] = (
-            send(part.at[k, 0, flat[3], :, front], diag_y.at[k], to_y),
-            send(part.at[k, 0, flat[3], :, back], diag_x.at[k], to_x),
-        )
-        plane_copies[k] = [
-            send(part.at[k, 0, flat[1], :, back], part_x.at[k, :, back], to_x),
-            send(part.at[k, 0, flat[2], :, front], part_y.at[k, :, front], to_y),
-        ]
+        diag, plane = [], []
+        for copy, columns, r, diag_to, partner, plane_to in (
+            (part_copies[k][0], front, 2, diag_y, to_y, part_y),
+            (part_copies[k][1], back, 1, diag_x, to_x, part_x),
+        ):
+            copy.wait_recv()
+
+            @pl.loop(0, 4)
+            def _(s):
+                part[k, 0, s, :, columns] = (
+                    part[k, 0, s, :, columns].astype(jnp.float32)
+                    + part_sib[k, s, :, columns].astype(jnp.float32)
+                ).astype(jnp.bfloat16)
+
+            diag.append(send(part.at[k, 0, flat[3], :, columns], diag_to.at[k], partner))
+            plane.append(
+                send(part.at[k, 0, flat[r], :, columns], plane_to.at[k, :, columns], partner)
+            )
+        diag_copies[k] = diag
+        plane_copies[k] = plane
 
     def give_plane(k):
         from_y, from_x = diag_copies[k]

time: 86.7 us -> 85.8 us (0.990)
  the two profiles are of different devices: /device:TPU:25 before, /device:TPU:24 now
where the time goes in v6:
time: 85.8 us; the launch traced here: 85.6 us
  Pallas kernels  82.1 us (96%)
  local copies, waits for them, and re-layouts  1.57 us (2%)
  other arithmetic  1.28 us (1%)
    pallas_call x1, Pallas kernels, dense_shards(): pl.pallas_call(layer_kernel, out_shape=jax.ShapeDtypeStruct((TOK_DEV, wid...  82.1 us

profile of v6, /device:TPU:24, one launch (start us, length us, event | category | flops | bytes accessed | tf_op | source)
XLA Modules:
  0.0 85.6 jit_solution(9952262136719783243)
XLA Ops:
  0.7 1.3 %convert_bitcast_fusion.gains_hbm = f32[8,128]{1,0:T(8,128)} fusion(bf16[128,8]{0,1:T(8,128)(2,1)} %param.18), kind=kLoop, calls=%fused_computation | loop fusion | flops 1024 | bytes 6144 | tf_op jit(solution)/shard_map/convert_element_type | solution.py:630
  1.9 82.1 %shard_map.109 = bf16[16,4096]{1,0:T(8,128)(2,1)} custom-call(bf16[128,1024]{1,0:T(8,128)(2,1)} %queries_hbm.1, bf16[4,1152,256]{2,1,0:T(8,128)(2,1)} %bitcast.11, s32[1]{0:T(128)S(6)} %copy.13.prefix_len, s32[8,128]{1,0:T(8,128)} %bitcast.13, f32[8,128]{1,0:T(8,128)} %convert_bitcast_fusion.gains_hbm, bf16[1024,1024]{1,0:T(8,128)(2,1)} %proj_hbm.1, ...), custom_call_target="tpu_custom_call" | custom-call | tf_op jit(solution)/shard_map/pallas_call | solution.py:584
  84.1 1.6 %copy.14 = bf16[16,4096]{1,0:T(8,128)(2,1)} copy(bf16[16,4096]{1,0:T(8,128)(2,1)} %shard_map.109) | data formatting | bytes 262144
